TPU v7x, 256 devices: a whole 4x4x8 slice. The times are simulated.
256 devices in a mesh: dp: 32 (over x, z), vocab: 8 (over y, core).
Axes of the slice: x: 4, y: 4, z: 8, core: 2. Of those that a mesh axis runs over, the one named last changes fastest.
Arguments:
- hidden: bfloat16 [32, 16, 8192], P('dp', 'vocab'), may hold values from -48 to 48
- targets: int32 [32, 16], P('dp', 'vocab'), may hold values from 0 to 128255
- unembed: bfloat16 [128256, 8192], P(('dp', 'vocab')), may hold values from -3 to 3
- out_proj: bfloat16 [128256, 64], P(('dp', 'vocab')), may hold values from -6 to 6
- in_proj: bfloat16 [8192, 64], replicated, may hold values from -0.0625 to 0.0625
Outputs:
- gradients: float32 [32, 4096], P('dp', 'vocab')
All inputs are finite; a program needn't handle non-finite values.
Results may differ from a plain program's by a relative error of at most 0.0003.
The roundings to bfloat16 on the way count: a program that leaves them out, or rounds other values in their place, can miss the bound.
Values may be sent and summed in bfloat16 or wider, within the bound.
No kernel may reach another device: no remote copies, remote signals or barrier semaphores. Data moves between devices by JAX's collectives and lax.ppermute only.
A program may use at most 128 MiB of HBM per device.

v0:
```python
import jax
import jax.numpy as jnp
from jax import lax
from jax.sharding import PartitionSpec as P


def body(hidden, targets, unembed, out_proj, in_proj):
    examples_here, part_len, features = hidden.shape
    own_count = examples_here * part_len
    own_rows = hidden.reshape(own_count, features)
    own_ids = targets.reshape(own_count)
    vocab_here = unembed.shape[0]
    out_width = out_proj.shape[1]
    in_width = in_proj.shape[1]
    row_ids = lax.iota(jnp.int32, vocab_here) + lax.axis_index(("dp", "vocab")) * vocab_here

    def scores(piece_rows):
        return lax.dot_general(
            unembed, piece_rows, (((1,), (1,)), ((), ())), preferred_element_type=jnp.float32
        )

    logits = scores(
        (
            lax.all_gather(own_rows, ("dp", "vocab"), axis=0, tiled=True),
            lax.all_gather(own_ids, ("dp", "vocab"), axis=0, tiled=True),
        )[0]
    )
    piece_max = jnp.max(logits, axis=0)
    piece_sum = jnp.sum(jnp.exp(logits - piece_max[None, :]), axis=0)
    local_max = piece_max
    local_sum = piece_sum
    col_max = lax.pmax(local_max, ("dp", "vocab"))
    col_sum = lax.psum(local_sum * jnp.exp(local_max - col_max), ("dp", "vocab"))
    piece_max = col_max
    piece_sum = col_sum
    softmax_w = (
        jnp.exp(
            scores(lax.all_gather(own_rows, ("dp", "vocab"), axis=0, tiled=True))
            - piece_max[None, :]
        )
        / piece_sum[None, :]
    )
    onehot = (
        row_ids[:, None] == lax.all_gather(own_ids, ("dp", "vocab"), axis=0, tiled=True)[None, :]
    ).astype(jnp.float32)
    delta_rows = (softmax_w - onehot).astype(jnp.bfloat16)
    projected = lax.dot_general(
        out_proj, delta_rows, (((0,), (0,)), ((), ())), preferred_element_type=jnp.float32
    )
    proj_rows = jnp.dot(own_rows, in_proj, preferred_element_type=jnp.float32)
    own_coords = lax.psum_scatter(projected, ("dp", "vocab"), scatter_dimension=1, tiled=True)
    partial_grads = jnp.einsum(
        "oel,eli->eoi",
        own_coords.reshape(out_width, examples_here, part_len),
        proj_rows.reshape(examples_here, part_len, in_width),
        precision=lax.Precision.HIGHEST,
    )
    return lax.psum_scatter(
        partial_grads.reshape(examples_here, out_width * in_width),
        "vocab",
        scatter_dimension=1,
        tiled=True,
    )


def solution(mesh):
    return jax.shard_map(
        body,
        mesh=mesh,
        in_specs=(
            P("dp", "vocab", None),
            P("dp", "vocab"),
            P(("dp", "vocab"), None),
            P(("dp", "vocab"), None),
            P(),
        ),
        out_specs=P("dp", "vocab"),
        check_vma=False,
    )
```

profile of v0, /device:TPU:1, one launch (start us, length us, event | category | flops | bytes accessed | tf_op | source)
XLA Modules:
  0.0 602.0 jit_solution(11668192445768986157)
XLA Ops:
  6.5 0.0 copy-start
  6.5 0.0 all-gather.4.cloned.1.call-start
  6.5 1.5 copy.7
  8.1 0.0 all-gather.4.cloned.1.call-update
  8.1 0.0 all-reduce.4.cloned.1.call-start
  8.1 0.8 bitcast_dynamic-update-slice_fusion
  8.9 81.8 %all-reduce = s32[512]{0:T(512)S(1)} all-reduce(s32[512]{0:T(512)S(1)} %bitcast_dynamic-update-slice_fusion), channel_id=3, replica_groups=mesh['dp'=32,'vocab'=8] {'dp','vocab'}, use_global_device_ids=true, to_apply=%add | all-reduce | flops 512 | bytes 4096
  90.7 49.5 %all-gather.4.cloned.1.call-done = bf16[1,512,8192]{2,0,1:T(2,128)(2,1)} async-done(((bf16[1,2,8192]{2,0,1:T(2,128)(2,1)}), bf16[1,512,8192]{2,0,1:T(2,128)(2,1)}) %all-gather.4.cloned.1.call-update) | async-done | bytes 8388624 | tf_op jit(solution)/shard_map/all_gather | solution.py:38
  140.2 20.2 %fusion.8 = (f32[512]{0:T(512)S(1)}, f32[501,512]{1,0:T(8,128)S(1)}) fusion(bf16[501,8192]{1,0:T(8,128)(2,1)} %param.7, bf16[1,512,8192]{2,0,1:T(2,128)(2,1)} %all-gather.4.cloned.1.call-done), kind=kOutput, calls=%fused_computation.14 | convolution fusion | flops 4202948608 | bytes 17625088 | tf_op jit(solution)/shard_map/dot_general | solution.py:18
  160.4 74.4 %pmax.7 = f32[512]{0:T(512)S(1)} all-reduce(f32[512]{0:T(512)S(1)} %get-tuple-element.5), channel_id=1, replica_groups=mesh['dp'=32,'vocab'=8] {'dp','vocab'}, use_global_device_ids=true, to_apply=%region_1.0 | all-reduce | flops 512 | bytes 4096 | tf_op jit(solution)/shard_map/pmax | solution.py:32
  234.8 0.2 exponential_reduce_fusion
  235.0 73.7 %psum.7 = f32[512]{0:T(512)S(1)} all-reduce(f32[512]{0:T(512)S(1)} %exponential_multiply_fusion), channel_id=1, replica_groups=mesh['dp'=32,'vocab'=8] {'dp','vocab'}, use_global_device_ids=true, to_apply=%region_3.0 | all-reduce | flops 512 | bytes 4096 | tf_op jit(solution)/shard_map/psum | solution.py:33
  308.7 0.0 copy-done.2
  308.7 0.4 convolution_bitcast_fusion
  309.1 0.8 copy.8
  309.9 0.0 all-reduce.4.cloned.1.call-update
  309.9 0.0 reduce-scatter.4.cloned.1.call-start
  310.0 0.4 fusion.3
  310.4 245.2 %all-reduce.4.cloned.1.call-done = f32[64,512]{0,1:T(8,128)} async-done(((f32[64,512]{0,1:T(8,128)}), f32[64,512]{0,1:T(8,128)}) %all-reduce.4.cloned.1.call-update) | async-done | bytes 131088
  555.6 0.9 fusion.5
  556.6 3.4 reshape.35
  560.0 0.0 reduce-scatter.4.cloned.1.call-update
  560.0 33.8 %reduce-scatter.4.cloned.1.call-done = f32[512,1]{1,0:T(8,128)} async-done(((f32[4096,1]{1,0:T(8,128)}), f32[512,1]{1,0:T(8,128)}) %reduce-scatter.4.cloned.1.call-update) | async-done | bytes 2064
  593.8 1.6 copy.10
  (7 shorter events, 0.0 us)
Async XLA Ops:
  6.5 303.5 %copy-start = (bf16[8192,64]{0,1:T(8,128)(2,1)S(1)}, bf16[8192,64]{0,1:T(8,128)(2,1)}, u32[]{:S(2)}) copy-start(bf16[8192,64]{0,1:T(8,128)(2,1)} %param.9) | copy-start | bytes 3145732
  6.5 133.7 %all-gather.4.cloned.1.call-start = ((), (), s32[]{:S(2)}) async-start(), calls=%async_computation.1 | async-start | bytes 16842752 | tf_op jit(solution)/shard_map/all_gather | solution.py:38
  8.1 547.5 %all-reduce.4.cloned.1.call-start = ((), (), s32[]{:S(2)}) async-start(), calls=%async_computation.3 | async-start | bytes 524288
  90.7 218.0 %copy-start.2 = (bf16[501,64]{0,1:T(8,128)(2,1)S(1)}, bf16[501,64]{0,1:T(8,128)(2,1)}, u32[]{:S(2)}) copy-start(bf16[501,64]{0,1:T(8,128)(2,1)} %param.8) | copy-start | bytes 192388
  90.7 219.3 %copy-start.1 = (bf16[1,2,8192]{2,1,0:T(2,128)(2,1)S(1)}, bf16[1,2,8192]{2,1,0:T(2,128)(2,1)}, u32[]{:S(2)}) copy-start(bf16[1,2,8192]{2,1,0:T(2,128)(2,1)} %param.5) | copy-start | bytes 98308
  309.9 283.9 %reduce-scatter.4.cloned.1.call-start = ((), (), s32[]{:S(2)}) async-start(), calls=%async_computation.2 | async-start | bytes 2359296
Sparse Core Ops, SparseCore 0:
  11.1 129.0 all-gather.3
  310.1 245.5 all-reduce.3
  560.1 33.6 reduce-scatter.3
where the time goes:
time: 604 us; the launch traced here: 602 us
  waiting for transfers between devices  329 us (54%)
  blocking collectives  230 us (38%)
  matrix products  21.8 us (4%)
  between operations  13.2 us (2%)
  local copies, waits for them, and re-layouts  8.2 us (1%)
    unnamed x5, waiting for transfers between devices  279 us
    unnamed x1, blocking collectives  81.8 us
    pmax x1, blocking collectives, body(): col_max = lax.pmax(local_max, ('dp', 'vocab'))  74.4 us
    psum x1, blocking collectives, body(): lax.psum(local_sum * jnp.exp(local_max - col_max), ('dp', 'vocab'))  73.7 us
    all_gather x1, waiting for transfers between devices, body(): lax.all_gather(own_rows, ('dp', 'vocab'), axis=0, tiled=True)  49.5 us
    dot_general x1, matrix products, scores(): lax.dot_general(unembed, piece_rows, (((1,), (1,)), ((), ())), preferred_...  20.2 us
  transfers between devices with their start and end apart: 3, of which 3 were waited for; matrix products, arithmetic and copies ran while one was open for 0% of the time, Pallas kernels for 0%

commit v1 on v0

v1 whole, which is shorter than its diff:
```python
import jax
import jax.numpy as jnp
import numpy as np
from jax import lax
from jax.experimental import pallas as pl
from jax.experimental.pallas import tpu as pltpu
from jax.sharding import Mesh, PartitionSpec as P

NX, NZ, NY, NC = 4, 8, 4, 2
ALL = ("x", "z", "y", "c")
GRAN = 32
KSTEPS = 8


def device_index(x, z, y, c):
    return ((x % NX * NZ + z % NZ) * NY + y % NY) * NC + c


def shift_pairs(axes, shift):
    pairs = []
    for x in range(NX):
        for z in range(NZ):
            for y in range(NY):
                for c in range(NC):
                    dx, dy = (shift, 0) if axes[c] == "x" else (0, shift)
                    pairs.append((device_index(x + dx, z, y + dy, c), device_index(x, z, y, c)))
    return pairs


def from_shift(value, axes, shift):
    return lax.ppermute(value, ALL, shift_pairs(axes, shift))


def swap_core(value):
    return lax.ppermute(value, "c", [(0, 1), (1, 0)])


def scores_kernel(core, offsets, *refs):
    blocks = refs[:8]
    u_own, u_other, in_t, own_out, other_out, rows, sems = refs[8:]
    step = pl.program_id(0)
    vocab_here = u_own.shape[0]
    width = u_own.shape[1]

    def copies():
        return [
            pltpu.make_async_copy(
                blocks[b].at[pl.ds(g * GRAN, GRAN), :],
                rows.at[pl.ds(pl.multiple_of(offsets[2 * b + g], GRAN), GRAN), :],
                sems.at[2 * b + g],
            )
            for b in range(8)
            for g in range(2)
        ]

    @pl.when(step == 0)
    def _():
        for copy in copies():
            copy.start()
        for copy in copies():
            copy.wait()
        own_out[...] = jnp.zeros_like(own_out)
        other_out[...] = jnp.zeros_like(other_out)

    piece = rows[:, pl.ds(pl.multiple_of(step * width, width), width)]

    def dot(left):
        return lax.dot_general(left, piece, (((1,), (1,)), ((), ())), preferred_element_type=jnp.float32)

    own_out[:vocab_here, :] += dot(u_own[...])
    other_out[:vocab_here, :] += dot(u_other[...])
    projected = dot(in_t[...])
    base = own_out.shape[0] - projected.shape[0]
    own_out[base:, :] += projected
    other_out[base:, :] += projected


def partial_scores(core, offsets, blocks, unembed, u_other, in_t):
    vocab_here = unembed.shape[0]
    half = u_other.shape[1]
    width = half // KSTEPS
    count = GRAN * NX * NY
    in_width = in_t.shape[0]
    out_rows = -(-vocab_here // 8) * 8 + in_width
    out = jax.ShapeDtypeStruct((out_rows, count), jnp.float32)
    return pl.pallas_call(
        scores_kernel,
        grid_spec=pltpu.PrefetchScalarGridSpec(
            num_scalar_prefetch=2,
            grid=(KSTEPS,),
            in_specs=[pl.BlockSpec(memory_space=pl.ANY)] * 8
            + [
                pl.BlockSpec((vocab_here, width), lambda k, core, offsets: (0, core[0] * KSTEPS + k)),
                pl.BlockSpec((vocab_here, width), lambda k, core, offsets: (0, k)),
                pl.BlockSpec((in_width, width), lambda k, core, offsets: (0, core[0] * KSTEPS + k)),
            ],
            out_specs=[pl.BlockSpec((out_rows, count), lambda k, core, offsets: (0, 0))] * 2,
            scratch_shapes=[pltpu.VMEM((count, half), jnp.bfloat16), pltpu.SemaphoreType.DMA((16,))],
        ),
        out_shape=[out, out],
        compiler_params=pltpu.CompilerParams(vmem_limit_bytes=40 * 2**20),
        cost_estimate=pl.CostEstimate(flops=2 * 2 * vocab_here * count * half, bytes_accessed=2 * half * (2 * vocab_here + count), transcendentals=0),
        name="partial_scores",
    )(core, offsets, *blocks, unembed, u_other, in_t)


def merge(pairs):
    top = jnp.max(pairs[:, 0], axis=0)
    total = jnp.sum(pairs[:, 1] * jnp.exp(pairs[:, 0] - top[None]), axis=0)
    return top, total


def body(hidden, targets, unembed, out_proj, in_proj):
    features = hidden.shape[2]
    half = features // 2
    vocab_here = unembed.shape[0]
    out_width = out_proj.shape[1]
    in_width = in_proj.shape[1]
    count = GRAN * NX * NY
    x, z, y, c = (lax.axis_index(a) for a in ALL)

    rows = hidden.reshape(2, features)
    keep = lax.dynamic_slice_in_dim(rows, c * half, half, 1)
    give = lax.dynamic_slice_in_dim(rows, (1 - c) * half, half, 1)
    got = swap_core(give)
    chip = jnp.where(c == 0, jnp.stack([keep, got]), jnp.stack([got, keep])).reshape(4, half)
    u_give = lax.dynamic_slice_in_dim(unembed, (1 - c) * half, half, 1)
    u_other = swap_core(u_give)

    along_z = lax.all_to_all(jnp.broadcast_to(chip[None], (NZ, 4, half)), "z", 0, 0)
    base = along_z.reshape(GRAN, half)

    first, second = ("x", "y"), ("y", "x")
    up = from_shift(base, first, 1)
    down = from_shift(base, first, -1)
    far = from_shift(base, first, 2)
    q1 = jnp.concatenate([base, up])
    q2 = jnp.concatenate([down, far])
    a = from_shift(q1, second, -1)
    b = from_shift(q2, second, 1)
    d = from_shift(q2, second, -1)
    e = from_shift(q1, second, 1)
    f = from_shift(a, second, -1)
    g = from_shift(b, second, 1)
    blocks = [q1, q2, a, b, d, e, f, g]
    places = [(0, 0), (1, 0), (0, -1), (1, 1), (1, -1), (0, 1), (0, 2), (1, 2)]
    p = jnp.where(c == 0, x, y)
    q = jnp.where(c == 0, y, x)
    offsets = []
    for which, s2 in places:
        for s1 in ((0, 1), (-1, 2))[which]:
            pp, qq = (p + s1) % 4, (q + s2) % 4
            xx, yy = jnp.where(c == 0, pp, qq), jnp.where(c == 0, qq, pp)
            offsets.append((xx * NY + yy) * GRAN)
    offsets = jnp.stack(offsets).astype(jnp.int32)
    core = c.astype(jnp.int32).reshape(1)
    own, other = partial_scores(core, offsets, blocks, unembed, u_other, in_proj.T)
    whole = own + swap_core(other)
    logits = whole[:vocab_here]
    proj = lax.dynamic_slice(
        whole[-in_width:].reshape(in_width, NX, NY, NZ, 4), (0, x, 0, z, 0), (in_width, 1, NY, 1, 4)
    ).reshape(in_width, 16)

    local_max = jnp.max(logits, axis=0)
    local_sum = jnp.sum(jnp.exp(logits - local_max[None, :]), axis=0)
    ids = jnp.pad(targets.reshape(2).astype(jnp.float32), (0, 126))
    message = jnp.concatenate([local_max, local_sum, ids])
    got = lax.all_to_all(jnp.broadcast_to(message[None], (NX * NY * NC, message.shape[0])), ("x", "y", "c"), 0, 0)
    top, total = merge(got[:, : 2 * count].reshape(-1, 2, count))
    ids = got[:, 2 * count : 2 * count + 2].reshape(64)
    message = jnp.concatenate([top, total, jnp.pad(ids, (0, 64))])
    got = lax.all_to_all(jnp.broadcast_to(message[None], (NZ, message.shape[0])), "z", 0, 0)
    col_max, col_sum = merge(got[:, : 2 * count].reshape(-1, 2, count))
    ids = got[:, 2 * count : 2 * count + 64].reshape(NZ, NX * NY, 4).transpose(1, 0, 2).reshape(count)
    ids = ids.astype(jnp.int32)

    row_ids = lax.iota(jnp.int32, vocab_here) + device_index(x, z, y, c) * vocab_here
    softmax_w = jnp.exp(logits - col_max[None, :]) / col_sum[None, :]
    onehot = (row_ids[:, None] == ids[None, :]).astype(jnp.float32)
    delta_rows = (softmax_w - onehot).astype(jnp.bfloat16)
    projected = lax.dot_general(
        out_proj, delta_rows, (((0,), (0,)), ((), ())), preferred_element_type=jnp.float32
    )
    sent = projected.reshape(8, 8, NX, NY, NZ, 4).transpose(2, 4, 0, 1, 3, 5).reshape(256, 128)
    got = lax.all_to_all(sent, ALL, 0, 0)
    coords = jnp.sum(got, axis=0).reshape(8, 16)
    grads = lax.dot_general(
        coords, proj, (((1,), (1,)), ((), ())), precision=lax.Precision.HIGHEST, preferred_element_type=jnp.float32
    )
    return grads.reshape(1, 8 * in_width)


def solution(mesh):
    wide = Mesh(np.asarray(mesh.devices).reshape(NX, NZ, NY, NC), ALL)
    dp, vocab = ("x", "z"), ("y", "c")
    return jax.shard_map(
        body,
        mesh=wide,
        in_specs=(
            P(dp, vocab, None),
            P(dp, vocab),
            P(ALL, None),
            P(ALL, None),
            P(),
        ),
        out_specs=P(dp, vocab),
        check_vma=False,
    )
```

time: 604 us -> 141 us (0.23)
  waiting for transfers between devices: 329 us -> 56.8 us
  blocking collectives: 230 us -> 18.5 us
  starting transfers between devices: 0.09 us -> 34.8 us
  matrix products: 21.8 us -> 0.52 us
  between operations: 13.2 us -> 0.26 us
  Pallas kernels: 0 us -> 11.9 us
  local copies, waits for them, and re-layouts: 8.2 us -> 16.9 us
    unnamed x5 -> x0, waiting for transfers between devices: 279 us -> none
    unnamed x1 -> x0, blocking collectives: 81.8 us -> none
    pmax x1 -> x0, blocking collectives: 74.4 us -> none  [body(): col_max = lax.pmax(local_max, ('dp', 'vocab'))]
    psum x1 -> x0, blocking collectives: 73.7 us -> none  [body(): lax.psum(local_sum * jnp.exp(local_max - col_max), ('dp', 'vocab'))]
    all_gather x1 -> x0, waiting for transfers between devices: 49.5 us -> none  [body(): lax.all_gather(own_rows, ('dp', 'vocab'), axis=0, tiled=True)]
    ppermute x0 -> x12, waiting for transfers between devices: none -> 29.3 us  [the longest x9 20.4 us: from_shift(): return lax.ppermute(value, ALL, shift_pairs(axes, shift))]
    all_to_all x0 -> x3, waiting for transfers between devices: none -> 27.6 us  [the longest x1 12.8 us: body(): got = lax.all_to_all(sent, ALL, 0, 0)]
    dot_general x3 -> x1, matrix products: 21.5 us -> 0.13 us  [body(): lax.dot_general(coords, proj, (((1,), (1,)), ((), ())), precision=lax.Pre...]
  transfers between devices with their start and end apart: 3 -> 15, of which waited for: 3 -> 12; matrix products, arithmetic and copies ran while one was open for 0% -> 0% of each run, Pallas kernels for 0% -> 0%
where the time goes in v1:
time: 141 us
  waiting for transfers between devices  56.8 us (40%)
  starting transfers between devices  34.8 us (25%)
  blocking collectives  18.5 us (13%)
  local copies, waits for them, and re-layouts  16.9 us (12%)
  Pallas kernels  11.9 us (8%)
    ppermute x9, waiting for transfers between devices, from_shift(): return lax.ppermute(value, ALL, shift_pairs(axes, shift))  20.4 us
    all_to_all x1, blocking collectives, body(): lax.all_to_all(jnp.broadcast_to(chip[None], (NZ, 4, half)), 'z', 0, 0)  18.5 us
    ppermute x9, starting transfers between devices, from_shift(): return lax.ppermute(value, ALL, shift_pairs(axes, shift))  13.6 us
    all_to_all x1, waiting for transfers between devices, body(): got = lax.all_to_all(sent, ALL, 0, 0)  12.8 us
    pallas_call x1, Pallas kernels, partial_scores(): pl.pallas_call(scores_kernel, grid_spec=pltpu.PrefetchScalarGridSpec(num_...  11.9 us
    ppermute x3, waiting for transfers between devices, swap_core(): return lax.ppermute(value, 'c', [(0, 1), (1, 0)])  8.89 us
    all_to_all x1, waiting for transfers between devices, body(): lax.all_to_all(jnp.broadcast_to(message[None], (NX * NY * NC, message.sha...  7.8 us
    all_to_all x1, waiting for transfers between devices, body(): lax.all_to_all(jnp.broadcast_to(message[None], (NZ, message.shape[0])), '...  6.97 us
  transfers between devices with their start and end apart: 15, of which 12 were waited for; matrix products, arithmetic and copies ran while one was open for 0% of the time, Pallas kernels for 0%

profile of v1, /device:TPU:1, one launch (start us, length us, event | category | flops | bytes accessed | tf_op | source)
XLA Modules:
  0.0 140.7 jit_solution(5912274946450434309)
XLA Ops:
  0.0 4.6 %constant_dynamic-slice_fusion.1 = bf16[501,4096]{1,0:T(8,128)(2,1)} fusion(bf16[501,8192]{1,0:T(8,128)(2,1)} %refs_8_.1, s32[]{:T(128)S(6)} %select_n.269), kind=kLoop, calls=%fused_computation.29 | loop fusion | bytes 8208388 | tf_op jit(solution)/shard_map/dynamic_slice | solution.py:127
  4.6 3.2 %collective-permute-start.10 = (bf16[501,4096]{1,0:T(8,128)(2,1)}, bf16[501,4096]{1,0:T(8,128)(2,1)}, u32[]{:S(2)}, u32[]{:S(2)}) collective-permute-start(bf16[501,4096]{1,0:T(8,128)(2,1)} %constant_dynamic-slice_fusion.1), channel_id=1, source_target_pairs={{0,1},{1,0},{2,3},{3,2},{4,5},{5,4},{6,7},{7,6},{8,9},{9,8},{10,11... | collective-permute-start | bytes 12312584 | tf_op jit(solution)/shard_map/ppermute | solution.py:35
  8.0 6.4 %collective-permute-done = bf16[2,4096]{1,0:T(2,128)(2,1)S(1)} collective-permute-done((bf16[2,4096]{1,0:T(2,128)(2,1)S(1)}, bf16[2,4096]{1,0:T(2,128)(2,1)S(1)}, u32[]{:S(2)}, u32[]{:S(2)}) %collective-permute-start) | collective-permute-done | bytes 16416 | tf_op jit(solution)/shard_map/ppermute | solution.py:35
  14.6 18.5 %all_to_all.32 = bf16[8,4,4096]{2,1,0:T(4,128)(2,1)S(1)} all-to-all(bf16[8,4,4096]{2,1,0:T(4,128)(2,1)S(1)} %broadcast_in_dim.6), channel_id=1, replica_groups=mesh['x'=4,'z'=8,'y'=4,'c'=2] {'z'}, dimensions={0} | all-to-all | bytes 524288 | tf_op jit(solution)/shard_map/all_to_all | solution.py:130
  34.6 2.6 %collective-permute-start.3 = (bf16[32,4096]{1,0:T(8,128)(2,1)S(1)}, bf16[32,4096]{1,0:T(8,128)(2,1)S(1)}, u32[]{:S(2)}, u32[]{:S(2)}) collective-permute-start(bf16[32,4096]{1,0:T(8,128)(2,1)S(1)} %reshape.81), channel_id=1, source_target_pairs={{128,0},{5,1},{130,2},{7,3},{132,4},{1,5},{134,6},{3,7},{136,8},{1... | collective-permute-start | bytes 786440 | tf_op jit(solution)/shard_map/ppermute | solution.py:31
  40.1 4.0 %collective-permute-done.3 = bf16[32,4096]{1,0:T(8,128)(2,1)S(1)} collective-permute-done((bf16[32,4096]{1,0:T(8,128)(2,1)S(1)}, bf16[32,4096]{1,0:T(8,128)(2,1)S(1)}, u32[]{:S(2)}, u32[]{:S(2)}) %collective-permute-start.3) | collective-permute-done | bytes 262176 | tf_op jit(solution)/shard_map/ppermute | solution.py:31
  44.1 2.3 %collective-permute-start.5 = (bf16[64,4096]{1,0:T(8,128)(2,1)S(1)}, bf16[64,4096]{1,0:T(8,128)(2,1)S(1)}, u32[]{:S(2)}, u32[]{:S(2)}) collective-permute-start(bf16[64,4096]{1,0:T(8,128)(2,1)S(1)} %constant_dynamic-update-slice_fusion.2.refs_1_), channel_id=1, source_target_pairs={{2,0},{65,1},{4,2},{67,3},{6,4},{69,5},{0,6},{71,7},{10,8},{73,9},... | collective-permute-start | bytes 1572872 | tf_op jit(solution)/shard_map/ppermute | solution.py:31
  46.7 2.6 %collective-permute-start.7 = (bf16[64,4096]{1,0:T(8,128)(2,1)S(1)}, bf16[64,4096]{1,0:T(8,128)(2,1)}, u32[]{:S(2)}, u32[]{:S(2)}) collective-permute-start(bf16[64,4096]{1,0:T(8,128)(2,1)S(1)} %constant_dynamic-update-slice_fusion.refs_0_), channel_id=1, source_target_pairs={{2,0},{65,1},{4,2},{67,3},{6,4},{69,5},{0,6},{71,7},{10,8},{73,9},... | collective-permute-start | bytes 1572872 | tf_op jit(solution)/shard_map/ppermute | solution.py:31
  49.2 3.3 %collective-permute-done.5.refs_3_ = bf16[64,4096]{1,0:T(8,128)(2,1)S(1)} collective-permute-done((bf16[64,4096]{1,0:T(8,128)(2,1)S(1)}, bf16[64,4096]{1,0:T(8,128)(2,1)S(1)}, u32[]{:S(2)}, u32[]{:S(2)}) %collective-permute-start.5) | collective-permute-done | bytes 524320 | tf_op jit(solution)/shard_map/ppermute | solution.py:31
  52.5 3.4 %collective-permute-start.9 = (bf16[64,4096]{1,0:T(8,128)(2,1)S(1)}, bf16[64,4096]{1,0:T(8,128)(2,1)}, u32[]{:S(2)}, u32[]{:S(2)}) collective-permute-start(bf16[64,4096]{1,0:T(8,128)(2,1)S(1)} %collective-permute-done.5.refs_3_), channel_id=1, source_target_pairs={{2,0},{65,1},{4,2},{67,3},{6,4},{69,5},{0,6},{71,7},{10,8},{73,9},... | collective-permute-start | bytes 1572872 | tf_op jit(solution)/shard_map/ppermute | solution.py:31
  56.1 5.6 %collective-permute-done.6.refs_4_ = bf16[64,4096]{1,0:T(8,128)(2,1)} collective-permute-done((bf16[64,4096]{1,0:T(8,128)(2,1)S(1)}, bf16[64,4096]{1,0:T(8,128)(2,1)}, u32[]{:S(2)}, u32[]{:S(2)}) %collective-permute-start.6) | collective-permute-done | bytes 524320 | tf_op jit(solution)/shard_map/ppermute | solution.py:31
  61.7 2.1 %collective-permute-done.9.refs_7_ = bf16[64,4096]{1,0:T(8,128)(2,1)} collective-permute-done((bf16[64,4096]{1,0:T(8,128)(2,1)S(1)}, bf16[64,4096]{1,0:T(8,128)(2,1)}, u32[]{:S(2)}, u32[]{:S(2)}) %collective-permute-start.9) | collective-permute-done | bytes 524320 | tf_op jit(solution)/shard_map/ppermute | solution.py:31
  63.8 3.5 %collective-permute-done.8.refs_6_ = bf16[64,4096]{1,0:T(8,128)(2,1)} collective-permute-done((bf16[64,4096]{1,0:T(8,128)(2,1)S(1)}, bf16[64,4096]{1,0:T(8,128)(2,1)}, u32[]{:S(2)}, u32[]{:S(2)}) %collective-permute-start.8) | collective-permute-done | bytes 524320 | tf_op jit(solution)/shard_map/ppermute | solution.py:31
  67.3 11.9 %partial_scores.1 = (f32[568,512]{1,0:T(8,128)S(1)}, f32[568,512]{1,0:T(8,128)S(1)}) custom-call(s32[1]{0:T(128)} %bitcast.core, s32[16]{0:T(128)S(1)} %stack.79.offsets, bf16[64,4096]{1,0:T(8,128)(2,1)S(1)} %constant_dynamic-update-slice_fusion.refs_0_, bf16[64,4096]{1,0:T(8,128)(2,1)S(1)} %constant_dynamic-update-slice_fusion.2.refs_1_, ...), custom_call_target="tpu_custom_call" | custom-call | flops 4202692608 | bytes 12402688 | tf_op jit(solution)/shard_map/partial_scores/pallas_call | solution.py:86
  79.2 2.9 %collective-permute-start.11 = (f32[568,512]{1,0:T(8,128)S(1)}, f32[568,512]{1,0:T(8,128)S(1)}, u32[]{:S(2)}, u32[]{:S(2)}) collective-permute-start(f32[568,512]{1,0:T(8,128)S(1)} %get-tuple-element.8), channel_id=1, source_target_pairs={{0,1},{1,0},{2,3},{3,2},{4,5},{5,4},{6,7},{7,6},{8,9},{9,8},{10,11... | collective-permute-start | bytes 3489800 | tf_op jit(solution)/shard_map/ppermute | solution.py:35
  82.1 2.4 %collective-permute-done.11 = f32[568,512]{1,0:T(8,128)S(1)} collective-permute-done((f32[568,512]{1,0:T(8,128)S(1)}, f32[568,512]{1,0:T(8,128)S(1)}, u32[]{:S(2)}, u32[]{:S(2)}) %collective-permute-start.11) | collective-permute-done | bytes 1163296 | tf_op jit(solution)/shard_map/ppermute | solution.py:35
  85.9 4.5 %all-to-all-start.1 = ((f32[32,1,1152]{2,1,0:T(1,128)}), f32[32,1,1152]{2,1,0:T(1,128)S(1)}, u32[]{:S(2)}, u32[]{:S(2)}) async-start(f32[32,1,1152]{2,1,0:T(1,128)} %broadcast_in_dim.7), calls=%async_computation.1 | async-start | bytes 294912 | tf_op jit(solution)/shard_map/all_to_all | solution.py:168
  90.4 7.8 %all-to-all-done.1 = f32[32,1,1152]{2,1,0:T(1,128)S(1)} async-done(((f32[32,1,1152]{2,1,0:T(1,128)}), f32[32,1,1152]{2,1,0:T(1,128)S(1)}, u32[]{:S(2)}, u32[]{:S(2)}) %all-to-all-start.1) | async-done | bytes 147488 | tf_op jit(solution)/shard_map/all_to_all | solution.py:168
  99.3 3.7 %all-to-all-start.2 = ((f32[8,1,1152]{2,1,0:T(1,128)}), f32[8,1,1152]{2,1,0:T(1,128)S(1)}, u32[]{:S(2)}, u32[]{:S(2)}) async-start(f32[8,1,1152]{2,1,0:T(1,128)} %broadcast_in_dim.8), calls=%async_computation.2 | async-start | bytes 73728 | tf_op jit(solution)/shard_map/all_to_all | solution.py:172
  103.0 7.0 %all-to-all-done.2 = f32[8,1,1152]{2,1,0:T(1,128)S(1)} async-done(((f32[8,1,1152]{2,1,0:T(1,128)}), f32[8,1,1152]{2,1,0:T(1,128)S(1)}, u32[]{:S(2)}, u32[]{:S(2)}) %all-to-all-start.2) | async-done | bytes 36896 | tf_op jit(solution)/shard_map/all_to_all | solution.py:172
  112.9 3.4 %copy.16 = f32[4,8,8,8,4,4]{2,1,0,5,4,3:T(8,128)} copy(f32[4,8,8,8,4,4]{3,2,5,1,4,0:T(8,128)} %bitcast.72) | data formatting | bytes 262144 | tf_op jit(solution)/shard_map/transpose | solution.py:184
  116.3 2.8 %all_to_all.26 = f32[256,1,128]{0,2,1:T(8,128)S(1)} reshape(f32[4,8,8,8,4,4]{2,1,0,5,4,3:T(8,128)} %copy.16) | data formatting | bytes 262144 | tf_op jit(solution)/shard_map/all_to_all | solution.py:185
  119.9 6.7 %all-to-all-start.3 = ((f32[256,1,128]{2,1,0:T(1,128)}), f32[256,1,128]{2,1,0:T(1,128)S(1)}, u32[]{:S(2)}, u32[]{:S(2)}) async-start(f32[256,1,128]{2,1,0:T(1,128)} %copy.17), calls=%async_computation.3 | async-start | bytes 262144 | tf_op jit(solution)/shard_map/all_to_all | solution.py:185
  126.8 12.8 %all-to-all-done.3 = f32[256,1,128]{2,1,0:T(1,128)S(1)} async-done(((f32[256,1,128]{2,1,0:T(1,128)}), f32[256,1,128]{2,1,0:T(1,128)S(1)}, u32[]{:S(2)}, u32[]{:S(2)}) %all-to-all-start.3) | async-done | bytes 131104 | tf_op jit(solution)/shard_map/all_to_all | solution.py:185
  (64 shorter events, 12.4 us)
Async XLA Ops:
  0.0 110.4 %copy-start = (bf16[501,64]{0,1:T(8,128)(2,1)S(1)}, bf16[501,64]{0,1:T(8,128)(2,1)}, u32[]{:S(2)}) copy-start(bf16[501,64]{0,1:T(8,128)(2,1)} %param.8) | copy-start | bytes 192388
  0.0 7.9 %copy-start.2 = (bf16[1,2,8192]{2,1,0:T(2,128)(2,1)S(1)}, bf16[1,2,8192]{2,1,0:T(2,128)(2,1)}, u32[]{:S(2)}) copy-start(bf16[1,2,8192]{2,1,0:T(2,128)(2,1)} %param.5) | copy-start | bytes 98308
  4.6 62.7 %collective-permute-start.10 = (bf16[501,4096]{1,0:T(8,128)(2,1)}, bf16[501,4096]{1,0:T(8,128)(2,1)}, u32[]{:S(2)}, u32[]{:S(2)}) collective-permute-start(bf16[501,4096]{1,0:T(8,128)(2,1)} %constant_dynamic-slice_fusion.1), channel_id=1, source_target_pairs={{0,1},{1,0},{2,3},{3,2},{4,5},{5,4},{6,7},{7,6},{8,9},{9,8},{10,11... | collective-permute-start | bytes 12312584 | tf_op jit(solution)/shard_map/ppermute | solution.py:35
  7.9 6.5 %collective-permute-start = (bf16[2,4096]{1,0:T(2,128)(2,1)S(1)}, bf16[2,4096]{1,0:T(2,128)(2,1)S(1)}, u32[]{:S(2)}, u32[]{:S(2)}) collective-permute-start(bf16[2,4096]{1,0:T(2,128)(2,1)S(1)} %get-tuple-element.13), channel_id=1, source_target_pairs={{0,1},{1,0},{2,3},{3,2},{4,5},{5,4},{6,7},{7,6},{8,9},{9,8},{10,11... | collective-permute-start | bytes 49160 | tf_op jit(solution)/shard_map/ppermute | solution.py:35
  33.2 34.1 %copy-start.1 = (bf16[8192,64]{0,1:T(8,128)(2,1)S(1)}, bf16[8192,64]{0,1:T(8,128)(2,1)}, u32[]{:S(2)}) copy-start(bf16[8192,64]{0,1:T(8,128)(2,1)} %param.9) | copy-start | bytes 3145732
  33.2 6.9 %collective-permute-start.2 = (bf16[32,4096]{1,0:T(8,128)(2,1)S(1)}, bf16[32,4096]{1,0:T(8,128)(2,1)S(1)}, u32[]{:S(2)}, u32[]{:S(2)}) collective-permute-start(bf16[32,4096]{1,0:T(8,128)(2,1)S(1)} %reshape.81), channel_id=1, source_target_pairs={{192,0},{7,1},{194,2},{1,3},{196,4},{3,5},{198,6},{5,7},{200,8},{1... | collective-permute-start | bytes 786440 | tf_op jit(solution)/shard_map/ppermute | solution.py:31
  34.6 9.5 %collective-permute-start.3 = (bf16[32,4096]{1,0:T(8,128)(2,1)S(1)}, bf16[32,4096]{1,0:T(8,128)(2,1)S(1)}, u32[]{:S(2)}, u32[]{:S(2)}) collective-permute-start(bf16[32,4096]{1,0:T(8,128)(2,1)S(1)} %reshape.81), channel_id=1, source_target_pairs={{128,0},{5,1},{130,2},{7,3},{132,4},{1,5},{134,6},{3,7},{136,8},{1... | collective-permute-start | bytes 786440 | tf_op jit(solution)/shard_map/ppermute | solution.py:31
  37.2 9.1 %collective-permute-start.1 = (bf16[32,4096]{1,0:T(8,128)(2,1)S(1)}, bf16[32,4096]{1,0:T(8,128)(2,1)S(1)}, u32[]{:S(2)}, u32[]{:S(2)}) collective-permute-start(bf16[32,4096]{1,0:T(8,128)(2,1)S(1)} %reshape.81), channel_id=1, source_target_pairs={{64,0},{3,1},{66,2},{5,3},{68,4},{7,5},{70,6},{1,7},{72,8},{11,9},... | collective-permute-start | bytes 786440 | tf_op jit(solution)/shard_map/ppermute | solution.py:31
  44.1 8.4 %collective-permute-start.5 = (bf16[64,4096]{1,0:T(8,128)(2,1)S(1)}, bf16[64,4096]{1,0:T(8,128)(2,1)S(1)}, u32[]{:S(2)}, u32[]{:S(2)}) collective-permute-start(bf16[64,4096]{1,0:T(8,128)(2,1)S(1)} %constant_dynamic-update-slice_fusion.2.refs_1_), channel_id=1, source_target_pairs={{2,0},{65,1},{4,2},{67,3},{6,4},{69,5},{0,6},{71,7},{10,8},{73,9},... | collective-permute-start | bytes 1572872 | tf_op jit(solution)/shard_map/ppermute | solution.py:31
  46.4 9.6 %collective-permute-start.4 = (bf16[64,4096]{1,0:T(8,128)(2,1)S(1)}, bf16[64,4096]{1,0:T(8,128)(2,1)S(1)}, u32[]{:S(2)}, u32[]{:S(2)}) collective-permute-start(bf16[64,4096]{1,0:T(8,128)(2,1)S(1)} %constant_dynamic-update-slice_fusion.refs_0_), channel_id=1, source_target_pairs={{6,0},{193,1},{0,2},{195,3},{2,4},{197,5},{4,6},{199,7},{14,8},{20... | collective-permute-start | bytes 1572872 | tf_op jit(solution)/shard_map/ppermute | solution.py:31
  46.5 15.2 %collective-permute-start.6 = (bf16[64,4096]{1,0:T(8,128)(2,1)S(1)}, bf16[64,4096]{1,0:T(8,128)(2,1)}, u32[]{:S(2)}, u32[]{:S(2)}) collective-permute-start(bf16[64,4096]{1,0:T(8,128)(2,1)S(1)} %constant_dynamic-update-slice_fusion.2.refs_1_), channel_id=1, source_target_pairs={{6,0},{193,1},{0,2},{195,3},{2,4},{197,5},{4,6},{199,7},{14,8},{20... | collective-permute-start | bytes 1572872 | tf_op jit(solution)/shard_map/ppermute | solution.py:31
  46.7 15.1 %collective-permute-start.7 = (bf16[64,4096]{1,0:T(8,128)(2,1)S(1)}, bf16[64,4096]{1,0:T(8,128)(2,1)}, u32[]{:S(2)}, u32[]{:S(2)}) collective-permute-start(bf16[64,4096]{1,0:T(8,128)(2,1)S(1)} %constant_dynamic-update-slice_fusion.refs_0_), channel_id=1, source_target_pairs={{2,0},{65,1},{4,2},{67,3},{6,4},{69,5},{0,6},{71,7},{10,8},{73,9},... | collective-permute-start | bytes 1572872 | tf_op jit(solution)/shard_map/ppermute | solution.py:31
  52.5 11.3 %collective-permute-start.9 = (bf16[64,4096]{1,0:T(8,128)(2,1)S(1)}, bf16[64,4096]{1,0:T(8,128)(2,1)}, u32[]{:S(2)}, u32[]{:S(2)}) collective-permute-start(bf16[64,4096]{1,0:T(8,128)(2,1)S(1)} %collective-permute-done.5.refs_3_), channel_id=1, source_target_pairs={{2,0},{65,1},{4,2},{67,3},{6,4},{69,5},{0,6},{71,7},{10,8},{73,9},... | collective-permute-start | bytes 1572872 | tf_op jit(solution)/shard_map/ppermute | solution.py:31
  56.0 11.3 %collective-permute-start.8 = (bf16[64,4096]{1,0:T(8,128)(2,1)S(1)}, bf16[64,4096]{1,0:T(8,128)(2,1)}, u32[]{:S(2)}, u32[]{:S(2)}) collective-permute-start(bf16[64,4096]{1,0:T(8,128)(2,1)S(1)} %collective-permute-done.4.refs_2_), channel_id=1, source_target_pairs={{6,0},{193,1},{0,2},{195,3},{2,4},{197,5},{4,6},{199,7},{14,8},{20... | collective-permute-start | bytes 1572872 | tf_op jit(solution)/shard_map/ppermute | solution.py:31
  67.3 14.8 %copy-start.3 = (s32[1,2]{1,0:T(1,128)S(1)}, s32[1,2]{1,0:T(1,128)}, u32[]{:S(2)}) copy-start(s32[1,2]{1,0:T(1,128)} %param.6) | copy-start | bytes 28
  79.2 5.4 %collective-permute-start.11 = (f32[568,512]{1,0:T(8,128)S(1)}, f32[568,512]{1,0:T(8,128)S(1)}, u32[]{:S(2)}, u32[]{:S(2)}) collective-permute-start(f32[568,512]{1,0:T(8,128)S(1)} %get-tuple-element.8), channel_id=1, source_target_pairs={{0,1},{1,0},{2,3},{3,2},{4,5},{5,4},{6,7},{7,6},{8,9},{9,8},{10,11... | collective-permute-start | bytes 3489800 | tf_op jit(solution)/shard_map/ppermute | solution.py:35
  85.9 12.4 %all-to-all-start.1 = ((f32[32,1,1152]{2,1,0:T(1,128)}), f32[32,1,1152]{2,1,0:T(1,128)S(1)}, u32[]{:S(2)}, u32[]{:S(2)}) async-start(f32[32,1,1152]{2,1,0:T(1,128)} %broadcast_in_dim.7), calls=%async_computation.1 | async-start | bytes 294912 | tf_op jit(solution)/shard_map/all_to_all | solution.py:168
  99.3 10.7 %all-to-all-start.2 = ((f32[8,1,1152]{2,1,0:T(1,128)}), f32[8,1,1152]{2,1,0:T(1,128)S(1)}, u32[]{:S(2)}, u32[]{:S(2)}) async-start(f32[8,1,1152]{2,1,0:T(1,128)} %broadcast_in_dim.8), calls=%async_computation.2 | async-start | bytes 73728 | tf_op jit(solution)/shard_map/all_to_all | solution.py:172
  119.9 19.7 %all-to-all-start.3 = ((f32[256,1,128]{2,1,0:T(1,128)}), f32[256,1,128]{2,1,0:T(1,128)S(1)}, u32[]{:S(2)}, u32[]{:S(2)}) async-start(f32[256,1,128]{2,1,0:T(1,128)} %copy.17), calls=%async_computation.3 | async-start | bytes 262144 | tf_op jit(solution)/shard_map/all_to_all | solution.py:185

commit v2 on v1

v2 whole, which is shorter than its diff:
```python
import jax
import jax.numpy as jnp
import numpy as np
from jax import lax
from jax.experimental import pallas as pl
from jax.experimental.pallas import tpu as pltpu
from jax.sharding import Mesh, PartitionSpec as P

NX, NZ, NY, NC = 4, 8, 4, 2
ALL = ("x", "z", "y", "c")
GRAN = 32
PIECE = GRAN // NC
SIDE = NX * NY * PIECE
BLOCK = 512
STEPS = 4
DIGITS = 128
CONTRACT_LAST = (((1,), (1,)), ((), ()))
CONTRACT_FIRST = (((0,), (0,)), ((), ()))
CONTRACT = (((1,), (0,)), ((), ()))
VMEM_SPEC = pl.BlockSpec(memory_space=pltpu.VMEM)
SMEM_SPEC = pl.BlockSpec(memory_space=pltpu.SMEM)
ANY_SPEC = pl.BlockSpec(memory_space=pl.ANY)
PLACES = (((0, 0), (1, 0)), ((-1, 0), (2, 0)))


def device_index(x, z, y, c):
    return ((x % NX * NZ + z % NZ) * NY + y % NY) * NC + c


def shift_pairs(axes, shift):
    pairs = []
    for x in range(NX):
        for z in range(NZ):
            for y in range(NY):
                for c in range(NC):
                    dx, dy = (shift, 0) if axes[c] == "x" else (0, shift)
                    pairs.append((device_index(x + dx, z, y + dy, c), device_index(x, z, y, c)))
    return pairs


def from_shift(value, axes, shift):
    return lax.ppermute(value, ALL, shift_pairs(axes, shift))


def swap_core(value):
    return lax.ppermute(value, "c", [(0, 1), (1, 0)])


def params(mib):
    return pltpu.CompilerParams(vmem_limit_bytes=mib * 2**20)


def scores_kernel(core, offsets, *refs):
    blocks = refs[:8]
    unembed, swapped, in_hbm, keep, give, ids, rows, u_own, u_other, in_t, row_sems, u_sems = refs[8:]
    vocab_here, half = u_own.shape
    width = half // STEPS
    in_width = in_t.shape[0]
    start = pl.multiple_of(core[0] * half, half)

    copies = []
    for k in range(STEPS):
        here = pl.ds(k * width, width)
        there = pl.ds(pl.multiple_of(start + k * width, width), width)
        cols = pl.ds(k * width, width + (DIGITS if k == STEPS - 1 else 0))
        group = [
            pltpu.make_async_copy(
                blocks[b].at[pl.ds(i * PIECE, PIECE), cols],
                rows.at[pl.ds(pl.multiple_of(offsets[4 * b + i], PIECE), PIECE), cols],
                row_sems.at[k, 4 * b + i],
            )
            for b in range(8)
            for i in range(4)
        ]
        group.append(pltpu.make_async_copy(unembed.at[:, there], u_own.at[:, here], u_sems.at[k, 0]))
        group.append(pltpu.make_async_copy(swapped.at[:, there], u_other.at[:, here], u_sems.at[k, 1]))
        group.append(pltpu.make_async_copy(in_hbm.at[:, there], in_t.at[:, here], u_sems.at[k, 2]))
        copies.append(group)
    for group in copies:
        for copy in group:
            copy.start()
    for k in range(STEPS):
        for copy in copies[k]:
            copy.wait()
        cols = slice(k * width, (k + 1) * width)
        mine, theirs = rows[:SIDE, cols], rows[SIDE:, cols]

        def put(left, right, *places):
            value = lax.dot_general(left, right, CONTRACT_LAST, preferred_element_type=jnp.float32)
            for out, base, first, size in places:
                if k == 0:
                    out[base : base + size, :] = value[first : first + size, :]
                else:
                    out[base : base + size, :] += value[first : first + size, :]

        proj = 2 * BLOCK
        both = jnp.concatenate([in_t[:, cols], u_own[:, cols]], axis=0)
        put(both, mine, (keep, 0, in_width, vocab_here), (keep, proj, 0, in_width), (give, proj + in_width, 0, in_width))
        put(both, theirs, (give, BLOCK, in_width, vocab_here), (give, proj, 0, in_width), (keep, proj + in_width, 0, in_width))
        put(u_other[:, cols], mine, (keep, BLOCK, 0, vocab_here))
        put(u_other[:, cols], theirs, (give, 0, 0, vocab_here))
    digit = lax.broadcasted_iota(jnp.int32, (8, DIGITS), 1)
    scale = jnp.where(digit == 0, 1.0, jnp.where(digit == 1, 256.0, jnp.where(digit == 2, 65536.0, 0.0)))
    ids[...] = lax.dot_general(
        scale.astype(jnp.bfloat16), rows[:SIDE, half:], CONTRACT_LAST, preferred_element_type=jnp.float32
    )


def partial_scores(core, offsets, blocks, unembed, swapped, in_t):
    vocab_here, features = unembed.shape
    half = features // 2
    in_width = in_t.shape[0]
    out = jax.ShapeDtypeStruct((2 * BLOCK + 2 * in_width, SIDE), jnp.float32)
    return pl.pallas_call(
        scores_kernel,
        in_specs=[SMEM_SPEC] * 2 + [ANY_SPEC] * 11,
        out_specs=[VMEM_SPEC] * 3,
        scratch_shapes=[
            pltpu.VMEM((2 * SIDE, half + DIGITS), jnp.bfloat16),
            pltpu.VMEM((vocab_here, half), jnp.bfloat16),
            pltpu.VMEM((vocab_here, half), jnp.bfloat16),
            pltpu.VMEM((in_width, half), jnp.bfloat16),
            pltpu.SemaphoreType.DMA((STEPS, 32)),
            pltpu.SemaphoreType.DMA((STEPS, 3)),
        ],
        out_shape=[out, out, jax.ShapeDtypeStruct((8, SIDE), jnp.float32)],
        compiler_params=params(40),
        cost_estimate=pl.CostEstimate(
            flops=2 * 2 * vocab_here * 2 * SIDE * half, bytes_accessed=2 * half * (2 * vocab_here + 2 * SIDE), transcendentals=0
        ),
        name="partial_scores",
    )(core, offsets, *blocks, unembed, swapped, in_t)


def stats_kernel(vocab_here, keep, got, logits, proj, message):
    proj[...] = keep[2 * BLOCK :, :] + got[2 * BLOCK :, :]
    top = None
    for b in range(2):
        part = slice(b * BLOCK, b * BLOCK + vocab_here)
        value = keep[part, :] + got[part, :]
        logits[part, :] = value
        here = jnp.max(value, axis=0, keepdims=True)
        top = here if top is None else jnp.maximum(top, here)
    total = jnp.zeros_like(top)
    for b in range(2):
        part = slice(b * BLOCK, b * BLOCK + vocab_here)
        total += jnp.sum(jnp.exp(logits[part, :] - top), axis=0, keepdims=True)
    lse = top + jnp.log(total)
    line = lax.broadcasted_iota(jnp.int32, message.shape, 0)
    message[...] = jnp.where(line % 2 == 0, lse[:, :128], lse[:, 128:])


def local_stats(keep, got, vocab_here):
    chips = NX * NY * NZ
    return pl.pallas_call(
        lambda *refs: stats_kernel(vocab_here, *refs),
        in_specs=[VMEM_SPEC] * 2,
        out_specs=[VMEM_SPEC] * 3,
        out_shape=[
            jax.ShapeDtypeStruct((2 * BLOCK, SIDE), jnp.float32),
            jax.ShapeDtypeStruct((keep.shape[0] - 2 * BLOCK, SIDE), jnp.float32),
            jax.ShapeDtypeStruct((2 * chips, 128), jnp.float32),
        ],
        compiler_params=params(12),
        name="local_stats",
    )(keep, got)


def delta_kernel(place, logits, got, ids, op_own, op_other, out, coords):
    vocab_here, width = op_own.shape
    chips = got.shape[0] // 2
    parts = jnp.concatenate([got[pl.ds(h, chips, stride=2), :] for h in range(2)], axis=1)
    top = jnp.max(parts, axis=0, keepdims=True)
    total = jnp.sum(jnp.exp(parts - top), axis=0, keepdims=True)
    ids = ids[:1, :].astype(jnp.int32)
    projected = jnp.zeros((width, SIDE), jnp.float32)
    row = lax.broadcasted_iota(jnp.int32, (vocab_here, SIDE), 0)
    for b, op in enumerate((op_own, op_other)):
        weight = jnp.exp(logits[b * BLOCK : b * BLOCK + vocab_here, :] - top) / total
        onehot = (row + place[b] == ids).astype(jnp.float32)
        delta = (weight - onehot).astype(jnp.bfloat16)
        projected += lax.dot_general(op[...], delta, CONTRACT_FIRST, preferred_element_type=jnp.float32)
    coords[:, :width] = projected.T
    lane = lax.broadcasted_iota(jnp.int32, (NZ, 128), 1)
    core = place[2]
    for x in range(NX):
        pieces = []
        for u in range(8):
            start = x * NY * PIECE + u * NZ
            pieces.append(coords[start : start + NZ, :])
        for r in range(8):
            line = jnp.concatenate([piece[:, 8 * r : 8 * r + 8] for piece in pieces] * 2, axis=1)
            out[r * 32 + x * NZ : r * 32 + (x + 1) * NZ, :] = jnp.where(lane // 64 == core, line, 0.0)


def delta_project(place, logits, got, ids, op_own, op_other):
    return pl.pallas_call(
        delta_kernel,
        in_specs=[SMEM_SPEC] + [VMEM_SPEC] * 5,
        out_specs=VMEM_SPEC,
        scratch_shapes=[pltpu.VMEM((SIDE, 128), jnp.float32)],
        out_shape=jax.ShapeDtypeStruct((256, 128), jnp.float32),
        compiler_params=params(12),
        name="delta_project",
    )(place, logits, got, ids, op_own, op_other)


def weights_kernel(place, proj, out):
    in_width = proj.shape[0] // 2
    core, x, z = place[0], place[1], place[2]
    lane = lax.broadcasted_iota(jnp.int32, (SIDE, 128), 1)
    t = lax.broadcasted_iota(jnp.int32, (SIDE, 128), 0)
    wanted = t == x * (NY * PIECE) + (lane // 8 % 8) * NZ + z
    mine = wanted & (lane // 64 == core)
    theirs = wanted & (lane // 64 != core)

    def pick(rows, chosen):
        return lax.dot_general(
            rows, chosen.astype(jnp.float32), CONTRACT, precision=lax.Precision.HIGHEST, preferred_element_type=jnp.float32
        )

    out[...] = pick(proj[:in_width, :], mine) + pick(proj[in_width:, :], theirs)


def finish_kernel(got, weights, out):
    in_width = weights.shape[0]
    total = jnp.sum(got[...], axis=0, keepdims=True)
    k = lax.broadcasted_iota(jnp.int32, (8, 128), 0)
    lane = lax.broadcasted_iota(jnp.int32, (8, 128), 1)
    spread = jnp.where(lane % 8 == k, jnp.broadcast_to(total, (8, 128)), 0.0)
    grads = lax.dot_general(
        spread, weights[...], CONTRACT_LAST, precision=lax.Precision.HIGHEST, preferred_element_type=jnp.float32
    )
    for i in range(8):
        out[:, i * in_width : (i + 1) * in_width] = grads[i : i + 1, :]


def own_weights(place, proj):
    return pl.pallas_call(
        weights_kernel,
        in_specs=[SMEM_SPEC, VMEM_SPEC],
        out_specs=VMEM_SPEC,
        out_shape=jax.ShapeDtypeStruct((proj.shape[0] // 2, 128), jnp.float32),
        compiler_params=params(8),
        name="own_weights",
    )(place, proj)


def finish(got, weights):
    return pl.pallas_call(
        finish_kernel,
        in_specs=[VMEM_SPEC] * 2,
        out_specs=VMEM_SPEC,
        out_shape=jax.ShapeDtypeStruct((1, 8 * weights.shape[0]), jnp.float32),
        compiler_params=params(8),
        name="finish",
    )(got, weights)


def body(hidden, targets, unembed, out_proj, in_proj):
    features = hidden.shape[2]
    half = features // 2
    vocab_here = unembed.shape[0]
    x, z, y, c = (lax.axis_index(a) for a in ALL)

    rows = hidden.reshape(2, features)
    ids = targets.reshape(2, 1)
    place = lax.broadcasted_iota(jnp.int32, (2, DIGITS), 1)
    digits = jnp.where(place == 0, ids % 256, jnp.where(place == 1, ids // 256 % 256, jnp.where(place == 2, ids // 65536, 0)))
    digits = digits.astype(jnp.bfloat16)
    keep = jnp.concatenate([lax.dynamic_slice_in_dim(rows, c * half, half, 1), digits], axis=1)
    give = jnp.concatenate([lax.dynamic_slice_in_dim(rows, (1 - c) * half, half, 1), digits], axis=1)
    got = swap_core(give)
    chip = jnp.where(c == 0, jnp.stack([keep, got]), jnp.stack([got, keep])).reshape(4, half + DIGITS)
    late_u, late_o, late_i, chip = lax.optimization_barrier((unembed, out_proj, in_proj, chip))

    along_z = lax.all_to_all(jnp.broadcast_to(chip[None], (NZ,) + chip.shape), "z", 0, 0)
    base = along_z.transpose(1, 0, 2).reshape(GRAN, half + DIGITS)

    swapped = swap_core(late_u)
    op_other = swap_core(late_o)
    in_t = late_i.T

    first, second = ("x", "y"), ("y", "x")
    up = from_shift(base, first, 1)
    down = from_shift(base, first, -1)
    far = from_shift(base, first, 2)
    q1 = jnp.concatenate([base, up])
    q2 = jnp.concatenate([down, far])
    a = from_shift(q1, second, -1)
    b = from_shift(q2, second, 1)
    d = from_shift(q2, second, -1)
    e = from_shift(q1, second, 1)
    f = from_shift(a, second, -1)
    g = from_shift(b, second, 1)
    blocks = [q1, q2, a, b, d, e, f, g]
    places = [(0, 0), (1, 0), (0, -1), (1, 1), (1, -1), (0, 1), (0, 2), (1, 2)]
    p = jnp.where(c == 0, x, y)
    q = jnp.where(c == 0, y, x)
    offsets = []
    for which, s2 in places:
        for s1 in ((0, 1), (-1, 2))[which]:
            pp, qq = (p + s1) % 4, (q + s2) % 4
            xx, yy = jnp.where(c == 0, pp, qq), jnp.where(c == 0, qq, pp)
            for side in range(NC):
                offsets.append(jnp.where(c == side, 0, SIDE) + (xx * NY + yy) * PIECE)
    offsets = jnp.stack(offsets).astype(jnp.int32)
    core = c.astype(jnp.int32).reshape(1)
    kept, given, ids = partial_scores(core, offsets, blocks, unembed, swapped, in_t)
    logits, proj, message = local_stats(kept, swap_core(given), vocab_here)

    got = lax.all_to_all(message, ("x", "y", "z"), 0, 0, tiled=True)
    weights = own_weights(jnp.stack([c, x, z]).astype(jnp.int32), proj)
    device = device_index(x, z, y, c)
    other = device_index(x, z, y, 1 - c)
    place = jnp.stack([device * vocab_here, other * vocab_here, c]).astype(jnp.int32)
    sent = delta_project(place, logits, got, ids, out_proj, op_other)
    got = lax.all_to_all(sent, ("y", "c", "x", "z"), 0, 0, tiled=True)
    return finish(got, weights)


def solution(mesh):
    wide = Mesh(np.asarray(mesh.devices).reshape(NX, NZ, NY, NC), ALL)
    dp, vocab = ("x", "z"), ("y", "c")
    return jax.shard_map(
        body,
        mesh=wide,
        in_specs=(
            P(dp, vocab, None),
            P(dp, vocab),
            P(ALL, None),
            P(ALL, None),
            P(),
        ),
        out_specs=P(dp, vocab),
        check_vma=False,
    )
```

time: 141 us -> 119 us (0.84)
  local copies, waits for them, and re-layouts: 16.9 us -> 1.41 us
  waiting for transfers between devices: 56.8 us -> 46 us
  Pallas kernels: 11.9 us -> 14.6 us
  starting transfers between devices: 34.8 us -> 37.1 us
    all_to_all x3 -> x2, waiting for transfers between devices: 27.6 us -> 21.6 us  [the longest x1 12.3 us: body(): got = lax.all_to_all(sent, ('y', 'c', 'x', 'z'), 0, 0, tiled=True)]
    ppermute x3 -> x4, waiting for transfers between devices: 8.89 us -> 4.22 us  [swap_core(): return lax.ppermute(value, 'c', [(0, 1), (1, 0)])]
    dynamic_slice x3 -> x1, local copies, waits for them, and re-layouts: 4.66 us -> 0.77 us  [body(): lax.dynamic_slice_in_dim(rows, c * half, half, 1)]
    all_to_all x2 -> x0, local copies, waits for them, and re-layouts: 3.54 us -> none  [body(): got = lax.all_to_all(sent, ALL, 0, 0)]
    transpose x1, local copies, waits for them, and re-layouts: 3.43 us -> 0.03 us  [body(): base = along_z.transpose(1, 0, 2).reshape(GRAN, half + DIGITS)]
    reshape x6 -> x0, local copies, waits for them, and re-layouts: 2.95 us -> none  [the longest x1 1.93 us: body(): projected.reshape(8, 8, NX, NY, NZ, 4).transpose(2, 4, 0, 1, 3, 5)]
    pallas_call x1 -> x5, Pallas kernels: 11.9 us -> 14.6 us  [the longest x1 9.62 us: partial_scores(): pl.pallas_call(scores_kernel, in_specs=[SMEM_SPEC] * 2 + [ANY_SPEC] * 11,...]
    all_to_all x3 -> x2, starting transfers between devices: 14.9 us -> 16.5 us  [the longest x1 9.82 us: body(): got = lax.all_to_all(message, ('x', 'y', 'z'), 0, 0, tiled=True)]
  transfers between devices with their start and end apart: 15 -> 15, of which waited for: 12 -> 13; matrix products, arithmetic and copies ran while one was open for 0% -> 1% of each run, Pallas kernels for 0% -> 1%
where the time goes in v2:
time: 119 us
  waiting for transfers between devices  46 us (39%)
  starting transfers between devices  37.1 us (31%)
  blocking collectives  18.7 us (16%)
  Pallas kernels  14.6 us (12%)
  local copies, waits for them, and re-layouts  1.41 us (1%)
    ppermute x9, waiting for transfers between devices, from_shift(): return lax.ppermute(value, ALL, shift_pairs(axes, shift))  20.2 us
    all_to_all x1, blocking collectives, body(): lax.all_to_all(jnp.broadcast_to(chip[None], (NZ,) + chip.shape), 'z', 0, 0)  18.7 us
    ppermute x9, starting transfers between devices, from_shift(): return lax.ppermute(value, ALL, shift_pairs(axes, shift))  13.1 us
    all_to_all x1, waiting for transfers between devices, body(): got = lax.all_to_all(sent, ('y', 'c', 'x', 'z'), 0, 0, tiled=True)  12.3 us
    all_to_all x1, starting transfers between devices, body(): got = lax.all_to_all(message, ('x', 'y', 'z'), 0, 0, tiled=True)  9.82 us
    pallas_call x1, Pallas kernels, partial_scores(): pl.pallas_call(scores_kernel, in_specs=[SMEM_SPEC] * 2 + [ANY_SPEC] * 11,...  9.62 us
    all_to_all x1, waiting for transfers between devices, body(): got = lax.all_to_all(message, ('x', 'y', 'z'), 0, 0, tiled=True)  9.33 us
    ppermute x4, starting transfers between devices, swap_core(): return lax.ppermute(value, 'c', [(0, 1), (1, 0)])  7.52 us
  transfers between devices with their start and end apart: 15, of which 13 were waited for; matrix products, arithmetic and copies ran while one was open for 1% of the time, Pallas kernels for 1%

profile of v2, /device:TPU:1, one launch (start us, length us, event | category | flops | bytes accessed | tf_op | source)
XLA Modules:
  0.0 119.0 jit_solution(11616039512493362541)
XLA Ops:
  1.6 3.3 %collective-permute-start = (bf16[2,4224]{1,0:T(2,128)(2,1)S(1)}, bf16[2,4224]{1,0:T(2,128)(2,1)S(1)}, u32[]{:S(2)}, u32[]{:S(2)}) collective-permute-start(bf16[2,4224]{1,0:T(2,128)(2,1)S(1)} %get-tuple-element.28), channel_id=1, source_target_pairs={{0,1},{1,0},{2,3},{3,2},{4,5},{5,4},{6,7},{7,6},{8,9},{9,8},{10,11... | collective-permute-start | bytes 50696 | tf_op jit(solution)/shard_map/ppermute | solution.py:46
  6.4 18.7 %all_to_all.27 = bf16[8,4,4224]{2,1,0:T(4,128)(2,1)S(1)} all-to-all(bf16[8,4,4224]{2,1,0:T(4,128)(2,1)S(1)} %broadcast_in_dim.32), channel_id=1, replica_groups=mesh['x'=4,'z'=8,'y'=4,'c'=2] {'z'}, dimensions={0} | all-to-all | bytes 540672 | tf_op jit(solution)/shard_map/all_to_all | solution.py:277
  25.1 2.8 %collective-permute-start.1 = (bf16[32,4224]{1,0:T(8,128)(2,1)S(1)}, bf16[32,4224]{1,0:T(8,128)(2,1)S(1)}, u32[]{:S(2)}, u32[]{:S(2)}) collective-permute-start(bf16[32,4224]{1,0:T(8,128)(2,1)S(1)} %bitcast.85), channel_id=1, source_target_pairs={{64,0},{3,1},{66,2},{5,3},{68,4},{7,5},{70,6},{1,7},{72,8},{11,9},... | collective-permute-start | bytes 811016 | tf_op jit(solution)/shard_map/ppermute | solution.py:42
  27.9 1.6 %collective-permute-start.3 = (bf16[32,4224]{1,0:T(8,128)(2,1)S(1)}, bf16[32,4224]{1,0:T(8,128)(2,1)S(1)}, u32[]{:S(2)}, u32[]{:S(2)}) collective-permute-start(bf16[32,4224]{1,0:T(8,128)(2,1)S(1)} %bitcast.87), channel_id=1, source_target_pairs={{128,0},{5,1},{130,2},{7,3},{132,4},{1,5},{134,6},{3,7},{136,8},{1... | collective-permute-start | bytes 811016 | tf_op jit(solution)/shard_map/ppermute | solution.py:42
  29.6 1.8 %collective-permute-done.1 = bf16[32,4224]{1,0:T(8,128)(2,1)S(1)} collective-permute-done((bf16[32,4224]{1,0:T(8,128)(2,1)S(1)}, bf16[32,4224]{1,0:T(8,128)(2,1)S(1)}, u32[]{:S(2)}, u32[]{:S(2)}) %collective-permute-start.1) | collective-permute-done | bytes 270368 | tf_op jit(solution)/shard_map/ppermute | solution.py:42
  31.3 1.3 %collective-permute-start.4 = (bf16[64,4224]{1,0:T(8,128)(2,1)S(1)}, bf16[64,4224]{1,0:T(8,128)(2,1)S(1)}, u32[]{:S(2)}, u32[]{:S(2)}) collective-permute-start(bf16[64,4224]{1,0:T(8,128)(2,1)S(1)} %pad_maximum_fusion.refs_0_), channel_id=1, source_target_pairs={{6,0},{193,1},{0,2},{195,3},{2,4},{197,5},{4,6},{199,7},{14,8},{20... | collective-permute-start | bytes 1622024 | tf_op jit(solution)/shard_map/ppermute | solution.py:42
  32.6 5.5 %collective-permute-done.2 = bf16[32,4224]{1,0:T(8,128)(2,1)S(1)} collective-permute-done((bf16[32,4224]{1,0:T(8,128)(2,1)S(1)}, bf16[32,4224]{1,0:T(8,128)(2,1)S(1)}, u32[]{:S(2)}, u32[]{:S(2)}) %collective-permute-start.2) | collective-permute-done | bytes 270368 | tf_op jit(solution)/shard_map/ppermute | solution.py:42
  38.2 1.7 %collective-permute-start.5 = (bf16[64,4224]{1,0:T(8,128)(2,1)S(1)}, bf16[64,4224]{1,0:T(8,128)(2,1)S(1)}, u32[]{:S(2)}, u32[]{:S(2)}) collective-permute-start(bf16[64,4224]{1,0:T(8,128)(2,1)S(1)} %constant_dynamic-update-slice_fusion.refs_1_), channel_id=1, source_target_pairs={{2,0},{65,1},{4,2},{67,3},{6,4},{69,5},{0,6},{71,7},{10,8},{73,9},... | collective-permute-start | bytes 1622024 | tf_op jit(solution)/shard_map/ppermute | solution.py:42
  39.9 2.7 %collective-permute-start.7 = (bf16[64,4224]{1,0:T(8,128)(2,1)S(1)}, bf16[64,4224]{1,0:T(8,128)(2,1)}, u32[]{:S(2)}, u32[]{:S(2)}) collective-permute-start(bf16[64,4224]{1,0:T(8,128)(2,1)S(1)} %pad_maximum_fusion.refs_0_), channel_id=1, source_target_pairs={{2,0},{65,1},{4,2},{67,3},{6,4},{69,5},{0,6},{71,7},{10,8},{73,9},... | collective-permute-start | bytes 1622024 | tf_op jit(solution)/shard_map/ppermute | solution.py:42
  42.6 1.6 %collective-permute-done.4.refs_2_ = bf16[64,4224]{1,0:T(8,128)(2,1)S(1)} collective-permute-done((bf16[64,4224]{1,0:T(8,128)(2,1)S(1)}, bf16[64,4224]{1,0:T(8,128)(2,1)S(1)}, u32[]{:S(2)}, u32[]{:S(2)}) %collective-permute-start.4) | collective-permute-done | bytes 540704 | tf_op jit(solution)/shard_map/ppermute | solution.py:42
  44.2 2.6 %collective-permute-done.5.refs_3_ = bf16[64,4224]{1,0:T(8,128)(2,1)S(1)} collective-permute-done((bf16[64,4224]{1,0:T(8,128)(2,1)S(1)}, bf16[64,4224]{1,0:T(8,128)(2,1)S(1)}, u32[]{:S(2)}, u32[]{:S(2)}) %collective-permute-start.5) | collective-permute-done | bytes 540704 | tf_op jit(solution)/shard_map/ppermute | solution.py:42
  46.8 2.9 %collective-permute-start.9 = (bf16[64,4224]{1,0:T(8,128)(2,1)S(1)}, bf16[64,4224]{1,0:T(8,128)(2,1)}, u32[]{:S(2)}, u32[]{:S(2)}) collective-permute-start(bf16[64,4224]{1,0:T(8,128)(2,1)S(1)} %collective-permute-done.5.refs_3_), channel_id=1, source_target_pairs={{2,0},{65,1},{4,2},{67,3},{6,4},{69,5},{0,6},{71,7},{10,8},{73,9},... | collective-permute-start | bytes 1622024 | tf_op jit(solution)/shard_map/ppermute | solution.py:42
  50.4 2.4 %collective-permute-done.7.refs_5_ = bf16[64,4224]{1,0:T(8,128)(2,1)} collective-permute-done((bf16[64,4224]{1,0:T(8,128)(2,1)S(1)}, bf16[64,4224]{1,0:T(8,128)(2,1)}, u32[]{:S(2)}, u32[]{:S(2)}) %collective-permute-start.7) | collective-permute-done | bytes 540704 | tf_op jit(solution)/shard_map/ppermute | solution.py:42
  52.7 3.4 %collective-permute-done.8.refs_6_ = bf16[64,4224]{1,0:T(8,128)(2,1)} collective-permute-done((bf16[64,4224]{1,0:T(8,128)(2,1)S(1)}, bf16[64,4224]{1,0:T(8,128)(2,1)}, u32[]{:S(2)}, u32[]{:S(2)}) %collective-permute-start.8) | collective-permute-done | bytes 540704 | tf_op jit(solution)/shard_map/ppermute | solution.py:42
  56.2 2.4 %collective-permute-done.9.refs_7_ = bf16[64,4224]{1,0:T(8,128)(2,1)} collective-permute-done((bf16[64,4224]{1,0:T(8,128)(2,1)S(1)}, bf16[64,4224]{1,0:T(8,128)(2,1)}, u32[]{:S(2)}, u32[]{:S(2)}) %collective-permute-start.9) | collective-permute-done | bytes 540704 | tf_op jit(solution)/shard_map/ppermute | solution.py:42
  58.5 9.6 %partial_scores.1 = (f32[1152,256]{1,0:T(8,128)S(1)}, f32[1152,256]{1,0:T(8,128)S(1)}, f32[8,256]{1,0:T(8,128)S(1)}) custom-call(s32[1]{0:T(128)} %bitcast.2.core, s32[32]{0:T(128)S(1)} %stack.171.offsets, bf16[64,4224]{1,0:T(8,128)(2,1)S(1)} %pad_maximum_fusion.refs_0_, bf16[64,4224]{1,0:T(8,128)(2,1)S(1)} %constant_dynamic-update-slice_fusion.refs_1_, ...), custom_call_target="tpu_custom_call" | custom-call | flops 4202692608 | bytes 12402688 | tf_op jit(solution)/shard_map/partial_scores/pallas_call | solution.py:114
  68.2 3.0 %collective-permute-start.11 = (f32[1152,256]{1,0:T(8,128)S(1)}, f32[1152,256]{1,0:T(8,128)S(1)}, u32[]{:S(2)}, u32[]{:S(2)}) collective-permute-start(f32[1152,256]{1,0:T(8,128)S(1)} %get-tuple-element.19), channel_id=1, source_target_pairs={{0,1},{1,0},{2,3},{3,2},{4,5},{5,4},{6,7},{7,6},{8,9},{9,8},{10,11... | collective-permute-start | bytes 3538952 | tf_op jit(solution)/shard_map/ppermute | solution.py:46
  71.2 2.5 %collective-permute-done.11.refs_1_ = f32[1152,256]{1,0:T(8,128)S(1)} collective-permute-done((f32[1152,256]{1,0:T(8,128)S(1)}, f32[1152,256]{1,0:T(8,128)S(1)}, u32[]{:S(2)}, u32[]{:S(2)}) %collective-permute-start.11) | collective-permute-done | bytes 1179680 | tf_op jit(solution)/shard_map/ppermute | solution.py:46
  73.7 1.0 local_stats.1
  74.7 9.8 %all-to-all-start.1 = ((f32[128,2,128]{2,1,0:T(2,128)}), f32[128,2,128]{2,1,0:T(2,128)S(1)}, u32[]{:S(2)}, u32[]{:S(2)}) async-start(f32[128,2,128]{2,1,0:T(2,128)} %bitcast.43), calls=%async_computation.1 | async-start | bytes 262144 | tf_op jit(solution)/shard_map/all_to_all | solution.py:312
  86.6 9.3 %all-to-all-done.1 = f32[128,2,128]{2,1,0:T(2,128)S(1)} async-done(((f32[128,2,128]{2,1,0:T(2,128)}), f32[128,2,128]{2,1,0:T(2,128)S(1)}, u32[]{:S(2)}, u32[]{:S(2)}) %all-to-all-start.1) | async-done | bytes 131104 | tf_op jit(solution)/shard_map/all_to_all | solution.py:312
  95.9 2.3 %delta_project.1 = f32[256,128]{1,0:T(8,128)} custom-call(s32[3]{0:T(128)S(1)} %pad_add_fusion.place, f32[1024,256]{1,0:T(8,128)S(1)} %get-tuple-element.20.logits, f32[256,128]{1,0:T(8,128)S(1)} %bitcast.82, f32[8,256]{1,0:T(8,128)S(1)} %get-tuple-element.22.ids, bf16[501,64]{1,0:T(8,128)(2,1)S(1)} %copy.10.op_own, ...), custom_call_target="tpu_custom_call" | custom-call | tf_op jit(solution)/shard_map/delta_project/pallas_call | solution.py:197
  98.2 6.7 %all-to-all-start.2 = ((f32[256,1,128]{2,1,0:T(1,128)}), f32[256,1,128]{2,1,0:T(1,128)S(1)}, u32[]{:S(2)}, u32[]{:S(2)}) async-start(f32[256,1,128]{2,1,0:T(1,128)} %bitcast.46), calls=%async_computation.2 | async-start | bytes 262144 | tf_op jit(solution)/shard_map/all_to_all | solution.py:318
  105.9 12.3 %all-to-all-done.2 = f32[256,1,128]{2,1,0:T(1,128)S(1)} async-done(((f32[256,1,128]{2,1,0:T(1,128)}), f32[256,1,128]{2,1,0:T(1,128)S(1)}, u32[]{:S(2)}, u32[]{:S(2)}) %all-to-all-start.2) | async-done | bytes 131104 | tf_op jit(solution)/shard_map/all_to_all | solution.py:318
  (34 shorter events, 7.6 us)
Async XLA Ops:
  1.6 4.2 %collective-permute-start = (bf16[2,4224]{1,0:T(2,128)(2,1)S(1)}, bf16[2,4224]{1,0:T(2,128)(2,1)S(1)}, u32[]{:S(2)}, u32[]{:S(2)}) collective-permute-start(bf16[2,4224]{1,0:T(2,128)(2,1)S(1)} %get-tuple-element.28), channel_id=1, source_target_pairs={{0,1},{1,0},{2,3},{3,2},{4,5},{5,4},{6,7},{7,6},{8,9},{9,8},{10,11... | collective-permute-start | bytes 50696 | tf_op jit(solution)/shard_map/ppermute | solution.py:46
  5.9 52.7 %collective-permute-start.10 = (bf16[501,8192]{1,0:T(8,128)(2,1)}, bf16[501,8192]{1,0:T(8,128)(2,1)}, u32[]{:S(2)}, u32[]{:S(2)}) collective-permute-start(bf16[501,8192]{1,0:T(8,128)(2,1)} %refs_8_.1), channel_id=1, source_target_pairs={{0,1},{1,0},{2,3},{3,2},{4,5},{5,4},{6,7},{7,6},{8,9},{9,8},{10,11... | collective-permute-start | bytes 24625160 | tf_op jit(solution)/shard_map/ppermute | solution.py:46
  25.1 33.5 %copy-start = (bf16[8192,64]{0,1:T(8,128)(2,1)S(1)}, bf16[8192,64]{0,1:T(8,128)(2,1)}, u32[]{:S(2)}) copy-start(bf16[8192,64]{0,1:T(8,128)(2,1)} %param.9) | copy-start | bytes 3145732
  25.1 6.2 %collective-permute-start.1 = (bf16[32,4224]{1,0:T(8,128)(2,1)S(1)}, bf16[32,4224]{1,0:T(8,128)(2,1)S(1)}, u32[]{:S(2)}, u32[]{:S(2)}) collective-permute-start(bf16[32,4224]{1,0:T(8,128)(2,1)S(1)} %bitcast.85), channel_id=1, source_target_pairs={{64,0},{3,1},{66,2},{5,3},{68,4},{7,5},{70,6},{1,7},{72,8},{11,9},... | collective-permute-start | bytes 811016 | tf_op jit(solution)/shard_map/ppermute | solution.py:42
  27.9 10.3 %collective-permute-start.2 = (bf16[32,4224]{1,0:T(8,128)(2,1)S(1)}, bf16[32,4224]{1,0:T(8,128)(2,1)S(1)}, u32[]{:S(2)}, u32[]{:S(2)}) collective-permute-start(bf16[32,4224]{1,0:T(8,128)(2,1)S(1)} %bitcast.86), channel_id=1, source_target_pairs={{192,0},{7,1},{194,2},{1,3},{196,4},{3,5},{198,6},{5,7},{200,8},{1... | collective-permute-start | bytes 811016 | tf_op jit(solution)/shard_map/ppermute | solution.py:42
  27.9 10.3 %collective-permute-start.3 = (bf16[32,4224]{1,0:T(8,128)(2,1)S(1)}, bf16[32,4224]{1,0:T(8,128)(2,1)S(1)}, u32[]{:S(2)}, u32[]{:S(2)}) collective-permute-start(bf16[32,4224]{1,0:T(8,128)(2,1)S(1)} %bitcast.87), channel_id=1, source_target_pairs={{128,0},{5,1},{130,2},{7,3},{132,4},{1,5},{134,6},{3,7},{136,8},{1... | collective-permute-start | bytes 811016 | tf_op jit(solution)/shard_map/ppermute | solution.py:42
  31.3 12.8 %collective-permute-start.4 = (bf16[64,4224]{1,0:T(8,128)(2,1)S(1)}, bf16[64,4224]{1,0:T(8,128)(2,1)S(1)}, u32[]{:S(2)}, u32[]{:S(2)}) collective-permute-start(bf16[64,4224]{1,0:T(8,128)(2,1)S(1)} %pad_maximum_fusion.refs_0_), channel_id=1, source_target_pairs={{6,0},{193,1},{0,2},{195,3},{2,4},{197,5},{4,6},{199,7},{14,8},{20... | collective-permute-start | bytes 1622024 | tf_op jit(solution)/shard_map/ppermute | solution.py:42
  38.2 8.6 %collective-permute-start.5 = (bf16[64,4224]{1,0:T(8,128)(2,1)S(1)}, bf16[64,4224]{1,0:T(8,128)(2,1)S(1)}, u32[]{:S(2)}, u32[]{:S(2)}) collective-permute-start(bf16[64,4224]{1,0:T(8,128)(2,1)S(1)} %constant_dynamic-update-slice_fusion.refs_1_), channel_id=1, source_target_pairs={{2,0},{65,1},{4,2},{67,3},{6,4},{69,5},{0,6},{71,7},{10,8},{73,9},... | collective-permute-start | bytes 1622024 | tf_op jit(solution)/shard_map/ppermute | solution.py:42
  39.9 10.4 %collective-permute-start.6 = (bf16[64,4224]{1,0:T(8,128)(2,1)S(1)}, bf16[64,4224]{1,0:T(8,128)(2,1)}, u32[]{:S(2)}, u32[]{:S(2)}) collective-permute-start(bf16[64,4224]{1,0:T(8,128)(2,1)S(1)} %constant_dynamic-update-slice_fusion.refs_1_), channel_id=1, source_target_pairs={{6,0},{193,1},{0,2},{195,3},{2,4},{197,5},{4,6},{199,7},{14,8},{20... | collective-permute-start | bytes 1622024 | tf_op jit(solution)/shard_map/ppermute | solution.py:42
  39.9 12.8 %collective-permute-start.7 = (bf16[64,4224]{1,0:T(8,128)(2,1)S(1)}, bf16[64,4224]{1,0:T(8,128)(2,1)}, u32[]{:S(2)}, u32[]{:S(2)}) collective-permute-start(bf16[64,4224]{1,0:T(8,128)(2,1)S(1)} %pad_maximum_fusion.refs_0_), channel_id=1, source_target_pairs={{2,0},{65,1},{4,2},{67,3},{6,4},{69,5},{0,6},{71,7},{10,8},{73,9},... | collective-permute-start | bytes 1622024 | tf_op jit(solution)/shard_map/ppermute | solution.py:42
  44.2 12.0 %collective-permute-start.8 = (bf16[64,4224]{1,0:T(8,128)(2,1)S(1)}, bf16[64,4224]{1,0:T(8,128)(2,1)}, u32[]{:S(2)}, u32[]{:S(2)}) collective-permute-start(bf16[64,4224]{1,0:T(8,128)(2,1)S(1)} %collective-permute-done.4.refs_2_), channel_id=1, source_target_pairs={{6,0},{193,1},{0,2},{195,3},{2,4},{197,5},{4,6},{199,7},{14,8},{20... | collective-permute-start | bytes 1622024 | tf_op jit(solution)/shard_map/ppermute | solution.py:42
  46.8 11.7 %collective-permute-start.9 = (bf16[64,4224]{1,0:T(8,128)(2,1)S(1)}, bf16[64,4224]{1,0:T(8,128)(2,1)}, u32[]{:S(2)}, u32[]{:S(2)}) collective-permute-start(bf16[64,4224]{1,0:T(8,128)(2,1)S(1)} %collective-permute-done.5.refs_3_), channel_id=1, source_target_pairs={{2,0},{65,1},{4,2},{67,3},{6,4},{69,5},{0,6},{71,7},{10,8},{73,9},... | collective-permute-start | bytes 1622024 | tf_op jit(solution)/shard_map/ppermute | solution.py:42
  68.2 5.5 %collective-permute-start.11 = (f32[1152,256]{1,0:T(8,128)S(1)}, f32[1152,256]{1,0:T(8,128)S(1)}, u32[]{:S(2)}, u32[]{:S(2)}) collective-permute-start(f32[1152,256]{1,0:T(8,128)S(1)} %get-tuple-element.19), channel_id=1, source_target_pairs={{0,1},{1,0},{2,3},{3,2},{4,5},{5,4},{6,7},{7,6},{8,9},{9,8},{10,11... | collective-permute-start | bytes 3538952 | tf_op jit(solution)/shard_map/ppermute | solution.py:46
  73.7 10.9 %copy-start.1 = (bf16[501,64]{0,1:T(8,128)(2,1)S(1)}, bf16[501,64]{0,1:T(8,128)(2,1)}, u32[]{:S(2)}) copy-start(bf16[501,64]{0,1:T(8,128)(2,1)} %param.8) | copy-start | bytes 192388
  74.7 21.3 %all-to-all-start.1 = ((f32[128,2,128]{2,1,0:T(2,128)}), f32[128,2,128]{2,1,0:T(2,128)S(1)}, u32[]{:S(2)}, u32[]{:S(2)}) async-start(f32[128,2,128]{2,1,0:T(2,128)} %bitcast.43), calls=%async_computation.1 | async-start | bytes 262144 | tf_op jit(solution)/shard_map/all_to_all | solution.py:312
  84.9 1.7 %collective-permute-start.12 = (bf16[501,64]{1,0:T(8,128)(2,1)S(1)}, bf16[501,64]{1,0:T(8,128)(2,1)S(1)}, u32[]{:S(2)}, u32[]{:S(2)}) collective-permute-start(bf16[501,64]{1,0:T(8,128)(2,1)S(1)} %copy.9), channel_id=1, source_target_pairs={{0,1},{1,0},{2,3},{3,2},{4,5},{5,4},{6,7},{7,6},{8,9},{9,8},{10,11... | collective-permute-start | bytes 192392 | tf_op jit(solution)/shard_map/ppermute | solution.py:46
  98.2 19.9 %all-to-all-start.2 = ((f32[256,1,128]{2,1,0:T(1,128)}), f32[256,1,128]{2,1,0:T(1,128)S(1)}, u32[]{:S(2)}, u32[]{:S(2)}) async-start(f32[256,1,128]{2,1,0:T(1,128)} %bitcast.46), calls=%async_computation.2 | async-start | bytes 262144 | tf_op jit(solution)/shard_map/all_to_all | solution.py:318

commit v3 on v2

--- a/solution.py
+++ b/solution.py
@@ -13,6 +13,8 @@
 SIDE = NX * NY * PIECE
 BLOCK = 512
 STEPS = 4
+SPLIT = 2
+AHEAD = 9
 DIGITS = 128
 CONTRACT_LAST = (((1,), (1,)), ((), ()))
 CONTRACT_FIRST = (((0,), (0,)), ((), ()))
@@ -51,39 +53,61 @@
 
 
 def scores_kernel(core, offsets, *refs):
-    blocks = refs[:8]
-    unembed, swapped, in_hbm, keep, give, ids, rows, u_own, u_other, in_t, row_sems, u_sems = refs[8:]
+    blocks = refs[:-12]
+    unembed, swapped, in_hbm, keep, give, ids, rows, u_own, u_other, in_t, row_sems, u_sems = refs[-12:]
+    pieces = [block.at[i] for block in blocks for i in range(block.shape[0])]
     vocab_here, half = u_own.shape
     width = half // STEPS
     in_width = in_t.shape[0]
     start = pl.multiple_of(core[0] * half, half)
 
-    copies = []
+    side = core[0]
+    row_copies = []
+    for part in range(SPLIT):
+        size = half // SPLIT
+        cols = pl.ds(part * size, size + (DIGITS if part == SPLIT - 1 else 0))
+        row_copies.append(
+            [
+                pltpu.make_async_copy(piece.at[:, :, cols], rows.at[:, offsets[i], :, cols], row_sems.at[part, i])
+                for i, piece in enumerate(pieces)
+            ]
+        )
+    u_copies = []
     for k in range(STEPS):
         here = pl.ds(k * width, width)
         there = pl.ds(pl.multiple_of(start + k * width, width), width)
-        cols = pl.ds(k * width, width + (DIGITS if k == STEPS - 1 else 0))
-        group = [
-            pltpu.make_async_copy(
-                blocks[b].at[pl.ds(i * PIECE, PIECE), cols],
-                rows.at[pl.ds(pl.multiple_of(offsets[4 * b + i], PIECE), PIECE), cols],
-                row_sems.at[k, 4 * b + i],
-            )
-            for b in range(8)
-            for i in range(4)
-        ]
-        group.append(pltpu.make_async_copy(unembed.at[:, there], u_own.at[:, here], u_sems.at[k, 0]))
-        group.append(pltpu.make_async_copy(swapped.at[:, there], u_other.at[:, here], u_sems.at[k, 1]))
-        group.append(pltpu.make_async_copy(in_hbm.at[:, there], in_t.at[:, here], u_sems.at[k, 2]))
-        copies.append(group)
-    for group in copies:
+        u_copies.append(
+            [
+                pltpu.make_async_copy(unembed.at[:, there], u_own.at[:, here], u_sems.at[k, 0]),
+                pltpu.make_async_copy(swapped.at[:, there], u_other.at[:, here], u_sems.at[k, 1]),
+                pltpu.make_async_copy(in_hbm.at[:, there], in_t.at[:, here], u_sems.at[k, 2]),
+            ]
+        )
+    order, last = [], []
+    for k in range(STEPS):
+        if k % (STEPS // SPLIT) == 0:
+            order.append(row_copies[k // (STEPS // SPLIT)])
+        order.append(u_copies[k])
+        last.append(len(order))
+    ahead = AHEAD
+    for group in order[:ahead]:
         for copy in group:
             copy.start()
+    ahead = min(ahead, len(order))
+    waited = 0
     for k in range(STEPS):
-        for copy in copies[k]:
-            copy.wait()
+        needed = last[k]
+        while ahead < min(len(order), needed + AHEAD - 1):
+            for copy in order[ahead]:
+                copy.start()
+            ahead += 1
+        while waited < needed:
+            for copy in order[waited]:
+                copy.wait()
+            waited += 1
         cols = slice(k * width, (k + 1) * width)
-        mine, theirs = rows[:SIDE, cols], rows[SIDE:, cols]
+        mine = rows[side, :, :, cols].reshape(SIDE, width)
+        theirs = rows[1 - side, :, :, cols].reshape(SIDE, width)
 
         def put(left, right, *places):
             value = lax.dot_general(left, right, CONTRACT_LAST, preferred_element_type=jnp.float32)
@@ -102,7 +126,7 @@
     digit = lax.broadcasted_iota(jnp.int32, (8, DIGITS), 1)
     scale = jnp.where(digit == 0, 1.0, jnp.where(digit == 1, 256.0, jnp.where(digit == 2, 65536.0, 0.0)))
     ids[...] = lax.dot_general(
-        scale.astype(jnp.bfloat16), rows[:SIDE, half:], CONTRACT_LAST, preferred_element_type=jnp.float32
+        scale.astype(jnp.bfloat16), rows[side, :, :, half:].reshape(SIDE, DIGITS), CONTRACT_LAST, preferred_element_type=jnp.float32
     )
 
 
@@ -113,14 +137,14 @@
     out = jax.ShapeDtypeStruct((2 * BLOCK + 2 * in_width, SIDE), jnp.float32)
     return pl.pallas_call(
         scores_kernel,
-        in_specs=[SMEM_SPEC] * 2 + [ANY_SPEC] * 11,
+        in_specs=[SMEM_SPEC] * 2 + [ANY_SPEC] * (len(blocks) + 3),
         out_specs=[VMEM_SPEC] * 3,
         scratch_shapes=[
-            pltpu.VMEM((2 * SIDE, half + DIGITS), jnp.bfloat16),
+            pltpu.VMEM((NC, NX * NY, PIECE, half + DIGITS), jnp.bfloat16),
             pltpu.VMEM((vocab_here, half), jnp.bfloat16),
             pltpu.VMEM((vocab_here, half), jnp.bfloat16),
             pltpu.VMEM((in_width, half), jnp.bfloat16),
-            pltpu.SemaphoreType.DMA((STEPS, 32)),
+            pltpu.SemaphoreType.DMA((SPLIT, 16)),
             pltpu.SemaphoreType.DMA((STEPS, 3)),
         ],
         out_shape=[out, out, jax.ShapeDtypeStruct((8, SIDE), jnp.float32)],
@@ -266,7 +290,7 @@
     rows = hidden.reshape(2, features)
     ids = targets.reshape(2, 1)
     place = lax.broadcasted_iota(jnp.int32, (2, DIGITS), 1)
-    digits = jnp.where(place == 0, ids % 256, jnp.where(place == 1, ids // 256 % 256, jnp.where(place == 2, ids // 65536, 0)))
+    digits = jnp.where(place == 0, ids & 255, jnp.where(place == 1, (ids >> 8) & 255, jnp.where(place == 2, ids >> 16, 0)))
     digits = digits.astype(jnp.bfloat16)
     keep = jnp.concatenate([lax.dynamic_slice_in_dim(rows, c * half, half, 1), digits], axis=1)
     give = jnp.concatenate([lax.dynamic_slice_in_dim(rows, (1 - c) * half, half, 1), digits], axis=1)
@@ -282,28 +306,34 @@
     in_t = late_i.T
 
     first, second = ("x", "y"), ("y", "x")
+    far = from_shift(base, first, 2)
     up = from_shift(base, first, 1)
     down = from_shift(base, first, -1)
-    far = from_shift(base, first, 2)
     q1 = jnp.concatenate([base, up])
     q2 = jnp.concatenate([down, far])
     a = from_shift(q1, second, -1)
-    b = from_shift(q2, second, 1)
+    e = from_shift(q1, second, 1)
+    b1 = from_shift(down, second, 1)
+    b2 = from_shift(far, second, 1)
     d = from_shift(q2, second, -1)
-    e = from_shift(q1, second, 1)
+    a, e = lax.optimization_barrier((a, e))
     f = from_shift(a, second, -1)
-    g = from_shift(b, second, 1)
-    blocks = [q1, q2, a, b, d, e, f, g]
-    places = [(0, 0), (1, 0), (0, -1), (1, 1), (1, -1), (0, 1), (0, 2), (1, 2)]
+    g1 = from_shift(b1, second, 1)
+    g2 = from_shift(b2, second, 1)
+    near, away = (0, 1), (-1, 2)
+    gathered = [
+        (q1, near, 0), (q2, away, 0), (a, near, -1), (e, near, 1), (b1, (-1,), 1), (b2, (2,), 1),
+        (d, away, -1), (f, near, 2), (g1, (-1,), 2), (g2, (2,), 2),
+    ]
+    blocks = [v.reshape(-1, NC, PIECE, v.shape[1]) for v, _, _ in gathered]
     p = jnp.where(c == 0, x, y)
     q = jnp.where(c == 0, y, x)
     offsets = []
-    for which, s2 in places:
-        for s1 in ((0, 1), (-1, 2))[which]:
+    for _, shifts, s2 in gathered:
+        for s1 in shifts:
             pp, qq = (p + s1) % 4, (q + s2) % 4
             xx, yy = jnp.where(c == 0, pp, qq), jnp.where(c == 0, qq, pp)
-            for side in range(NC):
-                offsets.append(jnp.where(c == side, 0, SIDE) + (xx * NY + yy) * PIECE)
+            offsets.append(xx * NY + yy)
     offsets = jnp.stack(offsets).astype(jnp.int32)
     core = c.astype(jnp.int32).reshape(1)
     kept, given, ids = partial_scores(core, offsets, blocks, unembed, swapped, in_t)

time: 119 us -> 115 us (0.966)
  waiting for transfers between devices: 46 us -> 42.2 us
    ppermute x9 -> x11, waiting for transfers between devices: 20.2 us -> 16.4 us  [from_shift(): return lax.ppermute(value, ALL, shift_pairs(axes, shift))]
    ppermute x9 -> x11, starting transfers between devices: 13.1 us -> 14.5 us  [from_shift(): return lax.ppermute(value, ALL, shift_pairs(axes, shift))]
  transfers between devices with their start and end apart: 15 -> 17, of which waited for: 13 -> 11; matrix products, arithmetic and copies ran while one was open for 1% -> 1% of each run, Pallas kernels for 1% -> 1%
where the time goes in v3:
time: 115 us
  waiting for transfers between devices  42.2 us (37%)
  starting transfers between devices  37.7 us (33%)
  blocking collectives  18.7 us (16%)
  Pallas kernels  13.8 us (12%)
  local copies, waits for them, and re-layouts  1.39 us (1%)
    all_to_all x1, blocking collectives, body(): lax.all_to_all(jnp.broadcast_to(chip[None], (NZ,) + chip.shape), 'z', 0, 0)  18.7 us
    ppermute x11, waiting for transfers between devices, from_shift(): return lax.ppermute(value, ALL, shift_pairs(axes, shift))  16.4 us
    ppermute x11, starting transfers between devices, from_shift(): return lax.ppermute(value, ALL, shift_pairs(axes, shift))  14.5 us
    all_to_all x1, waiting for transfers between devices, body(): got = lax.all_to_all(sent, ('y', 'c', 'x', 'z'), 0, 0, tiled=True)  12.3 us
    all_to_all x1, starting transfers between devices, body(): got = lax.all_to_all(message, ('x', 'y', 'z'), 0, 0, tiled=True)  9.83 us
    all_to_all x1, waiting for transfers between devices, body(): got = lax.all_to_all(message, ('x', 'y', 'z'), 0, 0, tiled=True)  9.33 us
    pallas_call x1, Pallas kernels, partial_scores(): pl.pallas_call(scores_kernel, in_specs=[SMEM_SPEC] * 2 + [ANY_SPEC] * (le...  8.78 us
    all_to_all x1, starting transfers between devices, body(): got = lax.all_to_all(sent, ('y', 'c', 'x', 'z'), 0, 0, tiled=True)  6.73 us
  transfers between devices with their start and end apart: 17, of which 11 were waited for; matrix products, arithmetic and copies ran while one was open for 1% of the time, Pallas kernels for 1%

profile of v3, /device:TPU:1, one launch (start us, length us, event | category | flops | bytes accessed | tf_op | source)
XLA Modules:
  0.0 115.0 jit_solution(926494353521774891)
XLA Ops:
  1.6 3.3 %collective-permute-start = (bf16[2,4224]{1,0:T(2,128)(2,1)S(1)}, bf16[2,4224]{1,0:T(2,128)(2,1)S(1)}, u32[]{:S(2)}, u32[]{:S(2)}) collective-permute-start(bf16[2,4224]{1,0:T(2,128)(2,1)S(1)} %get-tuple-element.32), channel_id=1, source_target_pairs={{0,1},{1,0},{2,3},{3,2},{4,5},{5,4},{6,7},{7,6},{8,9},{9,8},{10,11... | collective-permute-start | bytes 50696 | tf_op jit(solution)/shard_map/ppermute | solution.py:48
  6.4 18.7 %all_to_all.27 = bf16[8,4,4224]{2,1,0:T(4,128)(2,1)S(1)} all-to-all(bf16[8,4,4224]{2,1,0:T(4,128)(2,1)S(1)} %broadcast_in_dim.32), channel_id=1, replica_groups=mesh['x'=4,'z'=8,'y'=4,'c'=2] {'z'}, dimensions={0} | all-to-all | bytes 540672 | tf_op jit(solution)/shard_map/all_to_all | solution.py:301
  25.1 2.8 %collective-permute-start.1 = (bf16[32,4224]{1,0:T(8,128)(2,1)S(1)}, bf16[32,4224]{1,0:T(8,128)(2,1)S(1)}, u32[]{:S(2)}, u32[]{:S(2)}) collective-permute-start(bf16[32,4224]{1,0:T(8,128)(2,1)S(1)} %bitcast.64), channel_id=1, source_target_pairs={{64,0},{3,1},{66,2},{5,3},{68,4},{7,5},{70,6},{1,7},{72,8},{11,9},... | collective-permute-start | bytes 811016 | tf_op jit(solution)/shard_map/ppermute | solution.py:44
  27.9 1.6 %collective-permute-start.3 = (bf16[32,4224]{1,0:T(8,128)(2,1)S(1)}, bf16[32,4224]{1,0:T(8,128)(2,1)S(1)}, u32[]{:S(2)}, u32[]{:S(2)}) collective-permute-start(bf16[32,4224]{1,0:T(8,128)(2,1)S(1)} %bitcast.66), channel_id=1, source_target_pairs={{128,0},{5,1},{130,2},{7,3},{132,4},{1,5},{134,6},{3,7},{136,8},{1... | collective-permute-start | bytes 811016 | tf_op jit(solution)/shard_map/ppermute | solution.py:44
  29.5 1.8 %collective-permute-done.1 = bf16[32,4224]{1,0:T(8,128)(2,1)S(1)} collective-permute-done((bf16[32,4224]{1,0:T(8,128)(2,1)S(1)}, bf16[32,4224]{1,0:T(8,128)(2,1)S(1)}, u32[]{:S(2)}, u32[]{:S(2)}) %collective-permute-start.1) | collective-permute-done | bytes 270368 | tf_op jit(solution)/shard_map/ppermute | solution.py:44
  31.3 1.3 %collective-permute-start.4 = (bf16[64,4224]{1,0:T(8,128)(2,1)S(1)}, bf16[64,4224]{1,0:T(8,128)(2,1)S(1)}, u32[]{:S(2)}, u32[]{:S(2)}) collective-permute-start(bf16[64,4224]{1,0:T(8,128)(2,1)S(1)} %pad_maximum_fusion), channel_id=1, source_target_pairs={{6,0},{193,1},{0,2},{195,3},{2,4},{197,5},{4,6},{199,7},{14,8},{20... | collective-permute-start | bytes 1622024 | tf_op jit(solution)/shard_map/ppermute | solution.py:44
  32.6 1.5 %collective-permute-start.5 = (bf16[64,4224]{1,0:T(8,128)(2,1)S(1)}, bf16[64,4224]{1,0:T(8,128)(2,1)S(1)}, u32[]{:S(2)}, u32[]{:S(2)}) collective-permute-start(bf16[64,4224]{1,0:T(8,128)(2,1)S(1)} %pad_maximum_fusion), channel_id=1, source_target_pairs={{2,0},{65,1},{4,2},{67,3},{6,4},{69,5},{0,6},{71,7},{10,8},{73,9},... | collective-permute-start | bytes 1622024 | tf_op jit(solution)/shard_map/ppermute | solution.py:44
  34.1 4.1 %collective-permute-done.2 = bf16[32,4224]{1,0:T(8,128)(2,1)S(1)} collective-permute-done((bf16[32,4224]{1,0:T(8,128)(2,1)S(1)}, bf16[32,4224]{1,0:T(8,128)(2,1)S(1)}, u32[]{:S(2)}, u32[]{:S(2)}) %collective-permute-start.2) | collective-permute-done | bytes 270368 | tf_op jit(solution)/shard_map/ppermute | solution.py:44
  38.2 1.6 %collective-permute-start.8 = (bf16[64,4224]{1,0:T(8,128)(2,1)S(1)}, bf16[64,4224]{1,0:T(8,128)(2,1)}, u32[]{:S(2)}, u32[]{:S(2)}) collective-permute-start(bf16[64,4224]{1,0:T(8,128)(2,1)S(1)} %constant_dynamic-update-slice_fusion), channel_id=1, source_target_pairs={{6,0},{193,1},{0,2},{195,3},{2,4},{197,5},{4,6},{199,7},{14,8},{20... | collective-permute-start | bytes 1622024 | tf_op jit(solution)/shard_map/ppermute | solution.py:44
  41.0 3.6 %collective-permute-done.4 = bf16[64,4224]{1,0:T(8,128)(2,1)S(1)} collective-permute-done((bf16[64,4224]{1,0:T(8,128)(2,1)S(1)}, bf16[64,4224]{1,0:T(8,128)(2,1)S(1)}, u32[]{:S(2)}, u32[]{:S(2)}) %collective-permute-start.4) | collective-permute-done | bytes 540704 | tf_op jit(solution)/shard_map/ppermute | solution.py:44
  44.6 1.5 %collective-permute-start.9 = (bf16[64,4224]{1,0:T(8,128)(2,1)S(1)}, bf16[64,4224]{1,0:T(8,128)(2,1)}, u32[]{:S(2)}, u32[]{:S(2)}) collective-permute-start(bf16[64,4224]{1,0:T(8,128)(2,1)S(1)} %collective-permute-done.4), channel_id=1, source_target_pairs={{6,0},{193,1},{0,2},{195,3},{2,4},{197,5},{4,6},{199,7},{14,8},{20... | collective-permute-start | bytes 1622024 | tf_op jit(solution)/shard_map/ppermute | solution.py:44
  46.0 1.9 %collective-permute-start.10 = (bf16[32,4224]{1,0:T(8,128)(2,1)S(1)}, bf16[32,4224]{1,0:T(8,128)(2,1)}, u32[]{:S(2)}, u32[]{:S(2)}) collective-permute-start(bf16[32,4224]{1,0:T(8,128)(2,1)S(1)} %collective-permute-done.6), channel_id=1, source_target_pairs={{2,0},{65,1},{4,2},{67,3},{6,4},{69,5},{0,6},{71,7},{10,8},{73,9},... | collective-permute-start | bytes 811016 | tf_op jit(solution)/shard_map/ppermute | solution.py:44
  47.9 2.4 %collective-permute-done.7 = bf16[32,4224]{1,0:T(8,128)(2,1)} collective-permute-done((bf16[32,4224]{1,0:T(8,128)(2,1)S(1)}, bf16[32,4224]{1,0:T(8,128)(2,1)}, u32[]{:S(2)}, u32[]{:S(2)}) %collective-permute-start.7) | collective-permute-done | bytes 270368 | tf_op jit(solution)/shard_map/ppermute | solution.py:44
  50.3 1.2 %collective-permute-start.11 = (bf16[32,4224]{1,0:T(8,128)(2,1)}, bf16[32,4224]{1,0:T(8,128)(2,1)}, u32[]{:S(2)}, u32[]{:S(2)}) collective-permute-start(bf16[32,4224]{1,0:T(8,128)(2,1)} %collective-permute-done.7), channel_id=1, source_target_pairs={{2,0},{65,1},{4,2},{67,3},{6,4},{69,5},{0,6},{71,7},{10,8},{73,9},... | collective-permute-start | bytes 811016 | tf_op jit(solution)/shard_map/ppermute | solution.py:44
  51.6 1.6 %collective-permute-done.10 = bf16[32,4224]{1,0:T(8,128)(2,1)} collective-permute-done((bf16[32,4224]{1,0:T(8,128)(2,1)S(1)}, bf16[32,4224]{1,0:T(8,128)(2,1)}, u32[]{:S(2)}, u32[]{:S(2)}) %collective-permute-start.10) | collective-permute-done | bytes 270368 | tf_op jit(solution)/shard_map/ppermute | solution.py:44
  53.2 3.0 %collective-permute-done.11 = bf16[32,4224]{1,0:T(8,128)(2,1)} collective-permute-done((bf16[32,4224]{1,0:T(8,128)(2,1)}, bf16[32,4224]{1,0:T(8,128)(2,1)}, u32[]{:S(2)}, u32[]{:S(2)}) %collective-permute-start.11) | collective-permute-done | bytes 270368 | tf_op jit(solution)/shard_map/ppermute | solution.py:44
  56.2 8.8 %partial_scores.1 = (f32[1152,256]{1,0:T(8,128)S(1)}, f32[1152,256]{1,0:T(8,128)S(1)}, f32[8,256]{1,0:T(8,128)S(1)}) custom-call(s32[1]{0:T(128)} %bitcast.2.core, s32[16]{0:T(128)S(1)} %stack.107.offsets, bf16[2,2,16,4224]{3,2,1,0:T(8,128)(2,1)S(1)} %bitcast.56, bf16[2,2,16,4224]{3,2,1,0:T(8,128)(2,1)S(1)} %bitcast.57, ...), custom_call_target="tpu_custom_call" | custom-call | flops 4202692608 | bytes 12402688 | tf_op jit(solution)/shard_map/partial_scores/pallas_call | solution.py:138
  65.0 2.1 %collective-permute-start.13 = (f32[1152,256]{1,0:T(8,128)S(1)}, f32[1152,256]{1,0:T(8,128)S(1)}, u32[]{:S(2)}, u32[]{:S(2)}) collective-permute-start(f32[1152,256]{1,0:T(8,128)S(1)} %get-tuple-element.23), channel_id=1, source_target_pairs={{0,1},{1,0},{2,3},{3,2},{4,5},{5,4},{6,7},{7,6},{8,9},{9,8},{10,11... | collective-permute-start | bytes 3538952 | tf_op jit(solution)/shard_map/ppermute | solution.py:48
  67.1 2.5 %collective-permute-done.13.refs_1_ = f32[1152,256]{1,0:T(8,128)S(1)} collective-permute-done((f32[1152,256]{1,0:T(8,128)S(1)}, f32[1152,256]{1,0:T(8,128)S(1)}, u32[]{:S(2)}, u32[]{:S(2)}) %collective-permute-start.13) | collective-permute-done | bytes 1179680 | tf_op jit(solution)/shard_map/ppermute | solution.py:48
  70.6 9.8 %all-to-all-start.1 = ((f32[128,2,128]{2,1,0:T(2,128)}), f32[128,2,128]{2,1,0:T(2,128)S(1)}, u32[]{:S(2)}, u32[]{:S(2)}) async-start(f32[128,2,128]{2,1,0:T(2,128)} %bitcast.40), calls=%async_computation.1 | async-start | bytes 262144 | tf_op jit(solution)/shard_map/all_to_all | solution.py:342
  82.5 9.3 %all-to-all-done.1 = f32[128,2,128]{2,1,0:T(2,128)S(1)} async-done(((f32[128,2,128]{2,1,0:T(2,128)}), f32[128,2,128]{2,1,0:T(2,128)S(1)}, u32[]{:S(2)}, u32[]{:S(2)}) %all-to-all-start.1) | async-done | bytes 131104 | tf_op jit(solution)/shard_map/all_to_all | solution.py:342
  91.9 2.3 %delta_project.1 = f32[256,128]{1,0:T(8,128)} custom-call(s32[3]{0:T(128)S(1)} %pad_add_fusion.place, f32[1024,256]{1,0:T(8,128)S(1)} %get-tuple-element.24.logits, f32[256,128]{1,0:T(8,128)S(1)} %bitcast.61, f32[8,256]{1,0:T(8,128)S(1)} %get-tuple-element.26.ids, bf16[501,64]{1,0:T(8,128)(2,1)S(1)} %copy.13.op_own, ...), custom_call_target="tpu_custom_call" | custom-call | tf_op jit(solution)/shard_map/delta_project/pallas_call | solution.py:221
  94.2 6.7 %all-to-all-start.2 = ((f32[256,1,128]{2,1,0:T(1,128)}), f32[256,1,128]{2,1,0:T(1,128)S(1)}, u32[]{:S(2)}, u32[]{:S(2)}) async-start(f32[256,1,128]{2,1,0:T(1,128)} %bitcast.43), calls=%async_computation.2 | async-start | bytes 262144 | tf_op jit(solution)/shard_map/all_to_all | solution.py:348
  101.8 12.3 %all-to-all-done.2 = f32[256,1,128]{2,1,0:T(1,128)S(1)} async-done(((f32[256,1,128]{2,1,0:T(1,128)}), f32[256,1,128]{2,1,0:T(1,128)S(1)}, u32[]{:S(2)}, u32[]{:S(2)}) %all-to-all-start.2) | async-done | bytes 131104 | tf_op jit(solution)/shard_map/all_to_all | solution.py:348
  (38 shorter events, 9.3 us)
Async XLA Ops:
  1.6 4.2 %collective-permute-start = (bf16[2,4224]{1,0:T(2,128)(2,1)S(1)}, bf16[2,4224]{1,0:T(2,128)(2,1)S(1)}, u32[]{:S(2)}, u32[]{:S(2)}) collective-permute-start(bf16[2,4224]{1,0:T(2,128)(2,1)S(1)} %get-tuple-element.32), channel_id=1, source_target_pairs={{0,1},{1,0},{2,3},{3,2},{4,5},{5,4},{6,7},{7,6},{8,9},{9,8},{10,11... | collective-permute-start | bytes 50696 | tf_op jit(solution)/shard_map/ppermute | solution.py:48
  5.8 50.4 %collective-permute-start.12 = (bf16[501,8192]{1,0:T(8,128)(2,1)}, bf16[501,8192]{1,0:T(8,128)(2,1)}, u32[]{:S(2)}, u32[]{:S(2)}) collective-permute-start(bf16[501,8192]{1,0:T(8,128)(2,1)} %refs_10_.1), channel_id=1, source_target_pairs={{0,1},{1,0},{2,3},{3,2},{4,5},{5,4},{6,7},{7,6},{8,9},{9,8},{10,11... | collective-permute-start | bytes 24625160 | tf_op jit(solution)/shard_map/ppermute | solution.py:48
  25.1 31.2 %copy-start = (bf16[8192,64]{0,1:T(8,128)(2,1)S(1)}, bf16[8192,64]{0,1:T(8,128)(2,1)}, u32[]{:S(2)}) copy-start(bf16[8192,64]{0,1:T(8,128)(2,1)} %param.9) | copy-start | bytes 3145732
  25.1 6.2 %collective-permute-start.1 = (bf16[32,4224]{1,0:T(8,128)(2,1)S(1)}, bf16[32,4224]{1,0:T(8,128)(2,1)S(1)}, u32[]{:S(2)}, u32[]{:S(2)}) collective-permute-start(bf16[32,4224]{1,0:T(8,128)(2,1)S(1)} %bitcast.64), channel_id=1, source_target_pairs={{64,0},{3,1},{66,2},{5,3},{68,4},{7,5},{70,6},{1,7},{72,8},{11,9},... | collective-permute-start | bytes 811016 | tf_op jit(solution)/shard_map/ppermute | solution.py:44
  27.9 10.3 %collective-permute-start.2 = (bf16[32,4224]{1,0:T(8,128)(2,1)S(1)}, bf16[32,4224]{1,0:T(8,128)(2,1)S(1)}, u32[]{:S(2)}, u32[]{:S(2)}) collective-permute-start(bf16[32,4224]{1,0:T(8,128)(2,1)S(1)} %bitcast.65), channel_id=1, source_target_pairs={{192,0},{7,1},{194,2},{1,3},{196,4},{3,5},{198,6},{5,7},{200,8},{1... | collective-permute-start | bytes 811016 | tf_op jit(solution)/shard_map/ppermute | solution.py:44
  27.9 10.3 %collective-permute-start.3 = (bf16[32,4224]{1,0:T(8,128)(2,1)S(1)}, bf16[32,4224]{1,0:T(8,128)(2,1)S(1)}, u32[]{:S(2)}, u32[]{:S(2)}) collective-permute-start(bf16[32,4224]{1,0:T(8,128)(2,1)S(1)} %bitcast.66), channel_id=1, source_target_pairs={{128,0},{5,1},{130,2},{7,3},{132,4},{1,5},{134,6},{3,7},{136,8},{1... | collective-permute-start | bytes 811016 | tf_op jit(solution)/shard_map/ppermute | solution.py:44
  31.3 13.2 %collective-permute-start.4 = (bf16[64,4224]{1,0:T(8,128)(2,1)S(1)}, bf16[64,4224]{1,0:T(8,128)(2,1)S(1)}, u32[]{:S(2)}, u32[]{:S(2)}) collective-permute-start(bf16[64,4224]{1,0:T(8,128)(2,1)S(1)} %pad_maximum_fusion), channel_id=1, source_target_pairs={{6,0},{193,1},{0,2},{195,3},{2,4},{197,5},{4,6},{199,7},{14,8},{20... | collective-permute-start | bytes 1622024 | tf_op jit(solution)/shard_map/ppermute | solution.py:44
  32.6 12.0 %collective-permute-start.5 = (bf16[64,4224]{1,0:T(8,128)(2,1)S(1)}, bf16[64,4224]{1,0:T(8,128)(2,1)S(1)}, u32[]{:S(2)}, u32[]{:S(2)}) collective-permute-start(bf16[64,4224]{1,0:T(8,128)(2,1)S(1)} %pad_maximum_fusion), channel_id=1, source_target_pairs={{2,0},{65,1},{4,2},{67,3},{6,4},{69,5},{0,6},{71,7},{10,8},{73,9},... | collective-permute-start | bytes 1622024 | tf_op jit(solution)/shard_map/ppermute | solution.py:44
  38.2 13.4 %collective-permute-start.8 = (bf16[64,4224]{1,0:T(8,128)(2,1)S(1)}, bf16[64,4224]{1,0:T(8,128)(2,1)}, u32[]{:S(2)}, u32[]{:S(2)}) collective-permute-start(bf16[64,4224]{1,0:T(8,128)(2,1)S(1)} %constant_dynamic-update-slice_fusion), channel_id=1, source_target_pairs={{6,0},{193,1},{0,2},{195,3},{2,4},{197,5},{4,6},{199,7},{14,8},{20... | collective-permute-start | bytes 1622024 | tf_op jit(solution)/shard_map/ppermute | solution.py:44
  39.8 6.3 %collective-permute-start.6 = (bf16[32,4224]{1,0:T(8,128)(2,1)S(1)}, bf16[32,4224]{1,0:T(8,128)(2,1)S(1)}, u32[]{:S(2)}, u32[]{:S(2)}) collective-permute-start(bf16[32,4224]{1,0:T(8,128)(2,1)S(1)} %collective-permute-done.2), channel_id=1, source_target_pairs={{2,0},{65,1},{4,2},{67,3},{6,4},{69,5},{0,6},{71,7},{10,8},{73,9},... | collective-permute-start | bytes 811016 | tf_op jit(solution)/shard_map/ppermute | solution.py:44
  44.6 5.7 %collective-permute-start.7 = (bf16[32,4224]{1,0:T(8,128)(2,1)S(1)}, bf16[32,4224]{1,0:T(8,128)(2,1)}, u32[]{:S(2)}, u32[]{:S(2)}) collective-permute-start(bf16[32,4224]{1,0:T(8,128)(2,1)S(1)} %collective-permute-done.3), channel_id=1, source_target_pairs={{2,0},{65,1},{4,2},{67,3},{6,4},{69,5},{0,6},{71,7},{10,8},{73,9},... | collective-permute-start | bytes 811016 | tf_op jit(solution)/shard_map/ppermute | solution.py:44
  44.6 11.6 %collective-permute-start.9 = (bf16[64,4224]{1,0:T(8,128)(2,1)S(1)}, bf16[64,4224]{1,0:T(8,128)(2,1)}, u32[]{:S(2)}, u32[]{:S(2)}) collective-permute-start(bf16[64,4224]{1,0:T(8,128)(2,1)S(1)} %collective-permute-done.4), channel_id=1, source_target_pairs={{6,0},{193,1},{0,2},{195,3},{2,4},{197,5},{4,6},{199,7},{14,8},{20... | collective-permute-start | bytes 1622024 | tf_op jit(solution)/shard_map/ppermute | solution.py:44
  46.0 7.1 %collective-permute-start.10 = (bf16[32,4224]{1,0:T(8,128)(2,1)S(1)}, bf16[32,4224]{1,0:T(8,128)(2,1)}, u32[]{:S(2)}, u32[]{:S(2)}) collective-permute-start(bf16[32,4224]{1,0:T(8,128)(2,1)S(1)} %collective-permute-done.6), channel_id=1, source_target_pairs={{2,0},{65,1},{4,2},{67,3},{6,4},{69,5},{0,6},{71,7},{10,8},{73,9},... | collective-permute-start | bytes 811016 | tf_op jit(solution)/shard_map/ppermute | solution.py:44
  50.3 5.9 %collective-permute-start.11 = (bf16[32,4224]{1,0:T(8,128)(2,1)}, bf16[32,4224]{1,0:T(8,128)(2,1)}, u32[]{:S(2)}, u32[]{:S(2)}) collective-permute-start(bf16[32,4224]{1,0:T(8,128)(2,1)} %collective-permute-done.7), channel_id=1, source_target_pairs={{2,0},{65,1},{4,2},{67,3},{6,4},{69,5},{0,6},{71,7},{10,8},{73,9},... | collective-permute-start | bytes 811016 | tf_op jit(solution)/shard_map/ppermute | solution.py:44
  65.0 4.6 %collective-permute-start.13 = (f32[1152,256]{1,0:T(8,128)S(1)}, f32[1152,256]{1,0:T(8,128)S(1)}, u32[]{:S(2)}, u32[]{:S(2)}) collective-permute-start(f32[1152,256]{1,0:T(8,128)S(1)} %get-tuple-element.23), channel_id=1, source_target_pairs={{0,1},{1,0},{2,3},{3,2},{4,5},{5,4},{6,7},{7,6},{8,9},{9,8},{10,11... | collective-permute-start | bytes 3538952 | tf_op jit(solution)/shard_map/ppermute | solution.py:48
  69.6 10.9 %copy-start.1 = (bf16[501,64]{0,1:T(8,128)(2,1)S(1)}, bf16[501,64]{0,1:T(8,128)(2,1)}, u32[]{:S(2)}) copy-start(bf16[501,64]{0,1:T(8,128)(2,1)} %param.8) | copy-start | bytes 192388
  70.6 21.3 %all-to-all-start.1 = ((f32[128,2,128]{2,1,0:T(2,128)}), f32[128,2,128]{2,1,0:T(2,128)S(1)}, u32[]{:S(2)}, u32[]{:S(2)}) async-start(f32[128,2,128]{2,1,0:T(2,128)} %bitcast.40), calls=%async_computation.1 | async-start | bytes 262144 | tf_op jit(solution)/shard_map/all_to_all | solution.py:342
  80.8 1.7 %collective-permute-start.14 = (bf16[501,64]{1,0:T(8,128)(2,1)S(1)}, bf16[501,64]{1,0:T(8,128)(2,1)S(1)}, u32[]{:S(2)}, u32[]{:S(2)}) collective-permute-start(bf16[501,64]{1,0:T(8,128)(2,1)S(1)} %copy.12), channel_id=1, source_target_pairs={{0,1},{1,0},{2,3},{3,2},{4,5},{5,4},{6,7},{7,6},{8,9},{9,8},{10,11... | collective-permute-start | bytes 192392 | tf_op jit(solution)/shard_map/ppermute | solution.py:48
  94.2 19.9 %all-to-all-start.2 = ((f32[256,1,128]{2,1,0:T(1,128)}), f32[256,1,128]{2,1,0:T(1,128)S(1)}, u32[]{:S(2)}, u32[]{:S(2)}) async-start(f32[256,1,128]{2,1,0:T(1,128)} %bitcast.43), calls=%async_computation.2 | async-start | bytes 262144 | tf_op jit(solution)/shard_map/all_to_all | solution.py:348

commit v4 on v3

--- a/solution.py
+++ b/solution.py
@@ -13,8 +13,7 @@
 SIDE = NX * NY * PIECE
 BLOCK = 512
 STEPS = 4
-SPLIT = 2
-AHEAD = 9
+SPLIT = 1
 DIGITS = 128
 CONTRACT_LAST = (((1,), (1,)), ((), ()))
 CONTRACT_FIRST = (((0,), (0,)), ((), ()))
@@ -22,6 +21,7 @@
 VMEM_SPEC = pl.BlockSpec(memory_space=pltpu.VMEM)
 SMEM_SPEC = pl.BlockSpec(memory_space=pltpu.SMEM)
 ANY_SPEC = pl.BlockSpec(memory_space=pl.ANY)
+HBM_SPEC = pl.BlockSpec(memory_space=pltpu.HBM)
 PLACES = (((0, 0), (1, 0)), ((-1, 0), (2, 0)))
 
 
@@ -52,108 +52,134 @@
     return pltpu.CompilerParams(vmem_limit_bytes=mib * 2**20)
 
 
-def scores_kernel(core, offsets, *refs):
-    blocks = refs[:-12]
-    unembed, swapped, in_hbm, keep, give, ids, rows, u_own, u_other, in_t, row_sems, u_sems = refs[-12:]
+def fetch_kernel(core, unembed, swapped, in_hbm, u_own, u_other, in_t, sems):
+    half = u_own.shape[1]
+    there = pl.ds(pl.multiple_of(core[0] * half, half), half)
+    copies = [
+        pltpu.make_async_copy(source.at[:, there], target, sems.at[i])
+        for i, (source, target) in enumerate(((unembed, u_own), (swapped, u_other), (in_hbm, in_t)))
+    ]
+    for copy in copies:
+        copy.start()
+    for copy in copies:
+        copy.wait()
+
+
+def fetch_columns(core, unembed, swapped, in_t):
+    vocab_here, features = unembed.shape
+    half = features // 2
+    in_width = in_t.shape[0]
+    return pl.pallas_call(
+        fetch_kernel,
+        in_specs=[SMEM_SPEC] + [HBM_SPEC] * 3,
+        out_specs=[VMEM_SPEC] * 3,
+        scratch_shapes=[pltpu.SemaphoreType.DMA((3,))],
+        out_shape=[
+            jax.ShapeDtypeStruct((vocab_here, half), jnp.bfloat16),
+            jax.ShapeDtypeStruct((vocab_here, half), jnp.bfloat16),
+            jax.ShapeDtypeStruct((in_width, half), jnp.bfloat16),
+        ],
+        compiler_params=params(44),
+        cost_estimate=pl.CostEstimate(flops=0, bytes_accessed=4 * half * (2 * vocab_here + in_width), transcendentals=0),
+        name="fetch_columns",
+    )(core, unembed, swapped, in_t)
+
+
+def give_kernel(core, offsets, *refs):
+    blocks = refs[:-6]
+    u_own, u_other, in_t, give, rows, row_sems = refs[-6:]
     pieces = [block.at[i] for block in blocks for i in range(block.shape[0])]
     vocab_here, half = u_own.shape
     width = half // STEPS
     in_width = in_t.shape[0]
-    start = pl.multiple_of(core[0] * half, half)
-
     side = core[0]
-    row_copies = []
+    copies = []
     for part in range(SPLIT):
         size = half // SPLIT
         cols = pl.ds(part * size, size + (DIGITS if part == SPLIT - 1 else 0))
-        row_copies.append(
+        copies.append(
             [
                 pltpu.make_async_copy(piece.at[:, :, cols], rows.at[:, offsets[i], :, cols], row_sems.at[part, i])
                 for i, piece in enumerate(pieces)
             ]
         )
-    u_copies = []
-    for k in range(STEPS):
-        here = pl.ds(k * width, width)
-        there = pl.ds(pl.multiple_of(start + k * width, width), width)
-        u_copies.append(
-            [
-                pltpu.make_async_copy(unembed.at[:, there], u_own.at[:, here], u_sems.at[k, 0]),
-                pltpu.make_async_copy(swapped.at[:, there], u_other.at[:, here], u_sems.at[k, 1]),
-                pltpu.make_async_copy(in_hbm.at[:, there], in_t.at[:, here], u_sems.at[k, 2]),
-            ]
-        )
-    order, last = [], []
+    for group in copies:
+        for copy in group:
+            copy.start()
     for k in range(STEPS):
         if k % (STEPS // SPLIT) == 0:
-            order.append(row_copies[k // (STEPS // SPLIT)])
-        order.append(u_copies[k])
-        last.append(len(order))
-    ahead = AHEAD
-    for group in order[:ahead]:
-        for copy in group:
-            copy.start()
-    ahead = min(ahead, len(order))
-    waited = 0
+            for copy in copies[k // (STEPS // SPLIT)]:
+                copy.wait()
+        cols = slice(k * width, (k + 1) * width)
+        theirs = rows[1 - side, :, :, cols].reshape(SIDE, width)
+        both = jnp.concatenate([in_t[:, cols], u_own[:, cols]], axis=0)
+        put(k, both, theirs, (give, BLOCK, in_width, vocab_here), (give, 2 * BLOCK, 0, in_width))
+        put(k, u_other[:, cols], theirs, (give, 0, 0, vocab_here))
+
+
+def put(k, left, right, *places):
+    value = lax.dot_general(left, right, CONTRACT_LAST, preferred_element_type=jnp.float32)
+    for out, base, first, size in places:
+        if k == 0:
+            out[base : base + size, :] = value[first : first + size, :]
+        else:
+            out[base : base + size, :] += value[first : first + size, :]
+
+
+def keep_kernel(core, rows, u_own, u_other, in_t, keep, ids):
+    vocab_here, half = u_own.shape
+    width = half // STEPS
+    in_width = in_t.shape[0]
+    side = core[0]
     for k in range(STEPS):
-        needed = last[k]
-        while ahead < min(len(order), needed + AHEAD - 1):
-            for copy in order[ahead]:
-                copy.start()
-            ahead += 1
-        while waited < needed:
-            for copy in order[waited]:
-                copy.wait()
-            waited += 1
         cols = slice(k * width, (k + 1) * width)
         mine = rows[side, :, :, cols].reshape(SIDE, width)
-        theirs = rows[1 - side, :, :, cols].reshape(SIDE, width)
-
-        def put(left, right, *places):
-            value = lax.dot_general(left, right, CONTRACT_LAST, preferred_element_type=jnp.float32)
-            for out, base, first, size in places:
-                if k == 0:
-                    out[base : base + size, :] = value[first : first + size, :]
-                else:
-                    out[base : base + size, :] += value[first : first + size, :]
-
-        proj = 2 * BLOCK
         both = jnp.concatenate([in_t[:, cols], u_own[:, cols]], axis=0)
-        put(both, mine, (keep, 0, in_width, vocab_here), (keep, proj, 0, in_width), (give, proj + in_width, 0, in_width))
-        put(both, theirs, (give, BLOCK, in_width, vocab_here), (give, proj, 0, in_width), (keep, proj + in_width, 0, in_width))
-        put(u_other[:, cols], mine, (keep, BLOCK, 0, vocab_here))
-        put(u_other[:, cols], theirs, (give, 0, 0, vocab_here))
+        put(k, both, mine, (keep, 0, in_width, vocab_here), (keep, 2 * BLOCK, 0, in_width))
+        put(k, u_other[:, cols], mine, (keep, BLOCK, 0, vocab_here))
     digit = lax.broadcasted_iota(jnp.int32, (8, DIGITS), 1)
     scale = jnp.where(digit == 0, 1.0, jnp.where(digit == 1, 256.0, jnp.where(digit == 2, 65536.0, 0.0)))
     ids[...] = lax.dot_general(
-        scale.astype(jnp.bfloat16), rows[side, :, :, half:].reshape(SIDE, DIGITS), CONTRACT_LAST, preferred_element_type=jnp.float32
+        scale.astype(jnp.bfloat16),
+        rows[side, :, :, half:].reshape(SIDE, DIGITS),
+        CONTRACT_LAST,
+        preferred_element_type=jnp.float32,
     )
 
 
-def partial_scores(core, offsets, blocks, unembed, swapped, in_t):
-    vocab_here, features = unembed.shape
-    half = features // 2
-    in_width = in_t.shape[0]
-    out = jax.ShapeDtypeStruct((2 * BLOCK + 2 * in_width, SIDE), jnp.float32)
-    return pl.pallas_call(
-        scores_kernel,
-        in_specs=[SMEM_SPEC] * 2 + [ANY_SPEC] * (len(blocks) + 3),
-        out_specs=[VMEM_SPEC] * 3,
-        scratch_shapes=[
-            pltpu.VMEM((NC, NX * NY, PIECE, half + DIGITS), jnp.bfloat16),
-            pltpu.VMEM((vocab_here, half), jnp.bfloat16),
-            pltpu.VMEM((vocab_here, half), jnp.bfloat16),
-            pltpu.VMEM((in_width, half), jnp.bfloat16),
-            pltpu.SemaphoreType.DMA((SPLIT, 16)),
-            pltpu.SemaphoreType.DMA((STEPS, 3)),
+def keep_scores(core, rows, u_own, u_other, in_t):
+    vocab_here, half = u_own.shape
+    return pl.pallas_call(
+        keep_kernel,
+        in_specs=[SMEM_SPEC] + [VMEM_SPEC] * 4,
+        out_specs=[VMEM_SPEC] * 2,
+        out_shape=[
+            jax.ShapeDtypeStruct((2 * BLOCK + in_t.shape[0], SIDE), jnp.float32),
+            jax.ShapeDtypeStruct((8, SIDE), jnp.float32),
         ],
-        out_shape=[out, out, jax.ShapeDtypeStruct((8, SIDE), jnp.float32)],
-        compiler_params=params(40),
+        compiler_params=params(4),
+        cost_estimate=pl.CostEstimate(flops=2 * 2 * vocab_here * SIDE * half, bytes_accessed=2 * half * 2 * vocab_here, transcendentals=0),
+        name="keep_scores",
+    )(core, rows, u_own, u_other, in_t)
+
+
+def give_scores(core, offsets, blocks, u_own, u_other, in_t):
+    vocab_here, half = u_own.shape
+    return pl.pallas_call(
+        give_kernel,
+        in_specs=[SMEM_SPEC] * 2 + [ANY_SPEC] * len(blocks) + [VMEM_SPEC] * 3,
+        out_specs=[VMEM_SPEC] * 2,
+        scratch_shapes=[pltpu.SemaphoreType.DMA((SPLIT, 16))],
+        out_shape=[
+            jax.ShapeDtypeStruct((2 * BLOCK + in_t.shape[0], SIDE), jnp.float32),
+            jax.ShapeDtypeStruct((NC, NX * NY, PIECE, half + DIGITS), jnp.bfloat16),
+        ],
+        compiler_params=params(4),
         cost_estimate=pl.CostEstimate(
-            flops=2 * 2 * vocab_here * 2 * SIDE * half, bytes_accessed=2 * half * (2 * vocab_here + 2 * SIDE), transcendentals=0
+            flops=2 * 2 * vocab_here * SIDE * half, bytes_accessed=2 * half * (2 * vocab_here + 2 * SIDE), transcendentals=0
         ),
-        name="partial_scores",
-    )(core, offsets, *blocks, unembed, swapped, in_t)
+        name="give_scores",
+    )(core, offsets, *blocks, u_own, u_other, in_t)
 
 
 def stats_kernel(vocab_here, keep, got, logits, proj, message):
@@ -195,13 +221,13 @@
     chips = got.shape[0] // 2
     parts = jnp.concatenate([got[pl.ds(h, chips, stride=2), :] for h in range(2)], axis=1)
     top = jnp.max(parts, axis=0, keepdims=True)
-    total = jnp.sum(jnp.exp(parts - top), axis=0, keepdims=True)
+    scale = 1.0 / jnp.sum(jnp.exp(parts - top), axis=0, keepdims=True)
     ids = ids[:1, :].astype(jnp.int32)
     projected = jnp.zeros((width, SIDE), jnp.float32)
     row = lax.broadcasted_iota(jnp.int32, (vocab_here, SIDE), 0)
     for b, op in enumerate((op_own, op_other)):
-        weight = jnp.exp(logits[b * BLOCK : b * BLOCK + vocab_here, :] - top) / total
-        onehot = (row + place[b] == ids).astype(jnp.float32)
+        weight = jnp.exp(logits[b * BLOCK : b * BLOCK + vocab_here, :] - top) * scale
+        onehot = (row == ids - place[b]).astype(jnp.float32)
         delta = (weight - onehot).astype(jnp.bfloat16)
         projected += lax.dot_general(op[...], delta, CONTRACT_FIRST, preferred_element_type=jnp.float32)
     coords[:, :width] = projected.T
@@ -229,8 +255,7 @@
     )(place, logits, got, ids, op_own, op_other)
 
 
-def weights_kernel(place, proj, out):
-    in_width = proj.shape[0] // 2
+def weights_kernel(place, proj, proj_other, out):
     core, x, z = place[0], place[1], place[2]
     lane = lax.broadcasted_iota(jnp.int32, (SIDE, 128), 1)
     t = lax.broadcasted_iota(jnp.int32, (SIDE, 128), 0)
@@ -243,7 +268,7 @@
             rows, chosen.astype(jnp.float32), CONTRACT, precision=lax.Precision.HIGHEST, preferred_element_type=jnp.float32
         )
 
-    out[...] = pick(proj[:in_width, :], mine) + pick(proj[in_width:, :], theirs)
+    out[...] = pick(proj[...], mine) + pick(proj_other[...], theirs)
 
 
 def finish_kernel(got, weights, out):
@@ -259,15 +284,15 @@
         out[:, i * in_width : (i + 1) * in_width] = grads[i : i + 1, :]
 
 
-def own_weights(place, proj):
+def own_weights(place, proj, proj_other):
     return pl.pallas_call(
         weights_kernel,
-        in_specs=[SMEM_SPEC, VMEM_SPEC],
+        in_specs=[SMEM_SPEC] + [VMEM_SPEC] * 2,
         out_specs=VMEM_SPEC,
-        out_shape=jax.ShapeDtypeStruct((proj.shape[0] // 2, 128), jnp.float32),
+        out_shape=jax.ShapeDtypeStruct((proj.shape[0], 128), jnp.float32),
         compiler_params=params(8),
         name="own_weights",
-    )(place, proj)
+    )(place, proj, proj_other)
 
 
 def finish(got, weights):
@@ -292,9 +317,10 @@
     place = lax.broadcasted_iota(jnp.int32, (2, DIGITS), 1)
     digits = jnp.where(place == 0, ids & 255, jnp.where(place == 1, (ids >> 8) & 255, jnp.where(place == 2, ids >> 16, 0)))
     digits = digits.astype(jnp.bfloat16)
-    keep = jnp.concatenate([lax.dynamic_slice_in_dim(rows, c * half, half, 1), digits], axis=1)
-    give = jnp.concatenate([lax.dynamic_slice_in_dim(rows, (1 - c) * half, half, 1), digits], axis=1)
-    got = swap_core(give)
+    keep = lax.dynamic_slice_in_dim(rows, c * half, half, 1)
+    got = swap_core(lax.dynamic_slice_in_dim(rows, (1 - c) * half, half, 1))
+    keep = jnp.concatenate([keep, digits], axis=1)
+    got = jnp.pad(got, ((0, 0), (0, DIGITS)))
     chip = jnp.where(c == 0, jnp.stack([keep, got]), jnp.stack([got, keep])).reshape(4, half + DIGITS)
     late_u, late_o, late_i, chip = lax.optimization_barrier((unembed, out_proj, in_proj, chip))
 
@@ -336,11 +362,14 @@
             offsets.append(xx * NY + yy)
     offsets = jnp.stack(offsets).astype(jnp.int32)
     core = c.astype(jnp.int32).reshape(1)
-    kept, given, ids = partial_scores(core, offsets, blocks, unembed, swapped, in_t)
-    logits, proj, message = local_stats(kept, swap_core(given), vocab_here)
+    held = fetch_columns(core, unembed, swapped, in_t)
+    given, gathered = give_scores(core, offsets, blocks, *held)
+    got = swap_core(given)
+    kept, ids = keep_scores(core, gathered, *held)
+    logits, proj, message = local_stats(kept, got, vocab_here)
 
     got = lax.all_to_all(message, ("x", "y", "z"), 0, 0, tiled=True)
-    weights = own_weights(jnp.stack([c, x, z]).astype(jnp.int32), proj)
+    weights = own_weights(jnp.stack([c, x, z]).astype(jnp.int32), proj, swap_core(proj))
     device = device_index(x, z, y, c)
     other = device_index(x, z, y, 1 - c)
     place = jnp.stack([device * vocab_here, other * vocab_here, c]).astype(jnp.int32)

time: 115 us -> 111 us (0.965)
  waiting for transfers between devices: 42.2 us -> 33.3 us
  starting transfers between devices: 37.7 us -> 39.9 us
  Pallas kernels: 13.8 us -> 15.9 us
    ppermute x11, waiting for transfers between devices: 16.4 us -> 12.9 us  [from_shift(): return lax.ppermute(value, ALL, shift_pairs(axes, shift))]
    all_to_all x1, waiting for transfers between devices: 12.3 us -> 9.06 us  [body(): got = lax.all_to_all(sent, ('y', 'c', 'x', 'z'), 0, 0, tiled=True)]
    ppermute x4 -> x5, waiting for transfers between devices: 4.22 us -> 1.8 us  [swap_core(): return lax.ppermute(value, 'c', [(0, 1), (1, 0)])]
    ppermute x4 -> x5, starting transfers between devices: 6.57 us -> 8.79 us  [swap_core(): return lax.ppermute(value, 'c', [(0, 1), (1, 0)])]
    pallas_call x2 -> x4, Pallas kernels: 9.6 us -> 11.7 us  [the longest x1 4.87 us: give_scores(): pl.pallas_call(give_kernel, in_specs=[SMEM_SPEC] * 2 + [ANY_SPEC] * len(b...]
  transfers between devices with their start and end apart: 17 -> 18, of which waited for: 11 -> 10; matrix products, arithmetic and copies ran while one was open for 1% -> 1% of each run, Pallas kernels for 1% -> 6%
where the time goes in v4:
time: 111 us; the launch traced here: 110 us
  starting transfers between devices  39.9 us (36%)
  waiting for transfers between devices  33.3 us (30%)
  blocking collectives  18.7 us (17%)
  Pallas kernels  15.9 us (14%)
  local copies, waits for them, and re-layouts  1.41 us (1%)
    all_to_all x1, blocking collectives, body(): lax.all_to_all(jnp.broadcast_to(chip[None], (NZ,) + chip.shape), 'z', 0, 0)  18.7 us
    ppermute x11, starting transfers between devices, from_shift(): return lax.ppermute(value, ALL, shift_pairs(axes, shift))  14.5 us
    ppermute x11, waiting for transfers between devices, from_shift(): return lax.ppermute(value, ALL, shift_pairs(axes, shift))  12.9 us
    all_to_all x1, starting transfers between devices, body(): got = lax.all_to_all(message, ('x', 'y', 'z'), 0, 0, tiled=True)  9.85 us
    all_to_all x1, waiting for transfers between devices, body(): got = lax.all_to_all(message, ('x', 'y', 'z'), 0, 0, tiled=True)  9.59 us
    all_to_all x1, waiting for transfers between devices, body(): got = lax.all_to_all(sent, ('y', 'c', 'x', 'z'), 0, 0, tiled=True)  9.06 us
    ppermute x5, starting transfers between devices, swap_core(): return lax.ppermute(value, 'c', [(0, 1), (1, 0)])  8.79 us
    all_to_all x1, starting transfers between devices, body(): got = lax.all_to_all(sent, ('y', 'c', 'x', 'z'), 0, 0, tiled=True)  6.7 us
  transfers between devices with their start and end apart: 18, of which 10 were waited for; matrix products, arithmetic and copies ran while one was open for 1% of the time, Pallas kernels for 6%

profile of v4, /device:TPU:1, one launch (start us, length us, event | category | flops | bytes accessed | tf_op | source)
XLA Modules:
  0.0 110.4 jit_solution(1440427901657436031)
XLA Ops:
  0.8 3.3 %collective-permute-start = (bf16[2,4096]{1,0:T(2,128)(2,1)S(1)}, bf16[2,4096]{1,0:T(2,128)(2,1)S(1)}, u32[]{:S(2)}, u32[]{:S(2)}) collective-permute-start(bf16[2,4096]{1,0:T(2,128)(2,1)S(1)} %get-tuple-element.38), channel_id=1, source_target_pairs={{0,1},{1,0},{2,3},{3,2},{4,5},{5,4},{6,7},{7,6},{8,9},{9,8},{10,11... | collective-permute-start | bytes 49160 | tf_op jit(solution)/shard_map/ppermute | solution.py:48
  5.6 18.7 %all_to_all.27 = bf16[8,4,4224]{2,1,0:T(4,128)(2,1)S(1)} all-to-all(bf16[8,4,4224]{2,1,0:T(4,128)(2,1)S(1)} %broadcast_in_dim.32), channel_id=1, replica_groups=mesh['x'=4,'z'=8,'y'=4,'c'=2] {'z'}, dimensions={0} | all-to-all | bytes 540672 | tf_op jit(solution)/shard_map/all_to_all | solution.py:327
  24.3 2.8 %collective-permute-start.1 = (bf16[32,4224]{1,0:T(8,128)(2,1)S(1)}, bf16[32,4224]{1,0:T(8,128)(2,1)S(1)}, u32[]{:S(2)}, u32[]{:S(2)}) collective-permute-start(bf16[32,4224]{1,0:T(8,128)(2,1)S(1)} %bitcast.65), channel_id=1, source_target_pairs={{64,0},{3,1},{66,2},{5,3},{68,4},{7,5},{70,6},{1,7},{72,8},{11,9},... | collective-permute-start | bytes 811016 | tf_op jit(solution)/shard_map/ppermute | solution.py:44
  27.1 1.6 %collective-permute-start.3 = (bf16[32,4224]{1,0:T(8,128)(2,1)S(1)}, bf16[32,4224]{1,0:T(8,128)(2,1)S(1)}, u32[]{:S(2)}, u32[]{:S(2)}) collective-permute-start(bf16[32,4224]{1,0:T(8,128)(2,1)S(1)} %bitcast.67), channel_id=1, source_target_pairs={{128,0},{5,1},{130,2},{7,3},{132,4},{1,5},{134,6},{3,7},{136,8},{1... | collective-permute-start | bytes 811016 | tf_op jit(solution)/shard_map/ppermute | solution.py:44
  28.8 1.8 %collective-permute-done.1 = bf16[32,4224]{1,0:T(8,128)(2,1)S(1)} collective-permute-done((bf16[32,4224]{1,0:T(8,128)(2,1)S(1)}, bf16[32,4224]{1,0:T(8,128)(2,1)S(1)}, u32[]{:S(2)}, u32[]{:S(2)}) %collective-permute-start.1) | collective-permute-done | bytes 270368 | tf_op jit(solution)/shard_map/ppermute | solution.py:44
  30.6 1.3 %collective-permute-start.4 = (bf16[64,4224]{1,0:T(8,128)(2,1)S(1)}, bf16[64,4224]{1,0:T(8,128)(2,1)S(1)}, u32[]{:S(2)}, u32[]{:S(2)}) collective-permute-start(bf16[64,4224]{1,0:T(8,128)(2,1)S(1)} %pad_maximum_fusion), channel_id=1, source_target_pairs={{6,0},{193,1},{0,2},{195,3},{2,4},{197,5},{4,6},{199,7},{14,8},{20... | collective-permute-start | bytes 1622024 | tf_op jit(solution)/shard_map/ppermute | solution.py:44
  31.8 1.5 %collective-permute-start.5 = (bf16[64,4224]{1,0:T(8,128)(2,1)S(1)}, bf16[64,4224]{1,0:T(8,128)(2,1)S(1)}, u32[]{:S(2)}, u32[]{:S(2)}) collective-permute-start(bf16[64,4224]{1,0:T(8,128)(2,1)S(1)} %pad_maximum_fusion), channel_id=1, source_target_pairs={{2,0},{65,1},{4,2},{67,3},{6,4},{69,5},{0,6},{71,7},{10,8},{73,9},... | collective-permute-start | bytes 1622024 | tf_op jit(solution)/shard_map/ppermute | solution.py:44
  33.3 4.1 %collective-permute-done.2 = bf16[32,4224]{1,0:T(8,128)(2,1)S(1)} collective-permute-done((bf16[32,4224]{1,0:T(8,128)(2,1)S(1)}, bf16[32,4224]{1,0:T(8,128)(2,1)S(1)}, u32[]{:S(2)}, u32[]{:S(2)}) %collective-permute-start.2) | collective-permute-done | bytes 270368 | tf_op jit(solution)/shard_map/ppermute | solution.py:44
  37.4 1.6 %collective-permute-start.8 = (bf16[64,4224]{1,0:T(8,128)(2,1)S(1)}, bf16[64,4224]{1,0:T(8,128)(2,1)}, u32[]{:S(2)}, u32[]{:S(2)}) collective-permute-start(bf16[64,4224]{1,0:T(8,128)(2,1)S(1)} %constant_dynamic-update-slice_fusion), channel_id=1, source_target_pairs={{6,0},{193,1},{0,2},{195,3},{2,4},{197,5},{4,6},{199,7},{14,8},{20... | collective-permute-start | bytes 1622024 | tf_op jit(solution)/shard_map/ppermute | solution.py:44
  40.2 3.6 %collective-permute-done.4 = bf16[64,4224]{1,0:T(8,128)(2,1)S(1)} collective-permute-done((bf16[64,4224]{1,0:T(8,128)(2,1)S(1)}, bf16[64,4224]{1,0:T(8,128)(2,1)S(1)}, u32[]{:S(2)}, u32[]{:S(2)}) %collective-permute-start.4) | collective-permute-done | bytes 540704 | tf_op jit(solution)/shard_map/ppermute | solution.py:44
  43.8 1.5 %collective-permute-start.9 = (bf16[64,4224]{1,0:T(8,128)(2,1)S(1)}, bf16[64,4224]{1,0:T(8,128)(2,1)}, u32[]{:S(2)}, u32[]{:S(2)}) collective-permute-start(bf16[64,4224]{1,0:T(8,128)(2,1)S(1)} %collective-permute-done.4), channel_id=1, source_target_pairs={{6,0},{193,1},{0,2},{195,3},{2,4},{197,5},{4,6},{199,7},{14,8},{20... | collective-permute-start | bytes 1622024 | tf_op jit(solution)/shard_map/ppermute | solution.py:44
  45.3 1.9 %collective-permute-start.10 = (bf16[32,4224]{1,0:T(8,128)(2,1)S(1)}, bf16[32,4224]{1,0:T(8,128)(2,1)}, u32[]{:S(2)}, u32[]{:S(2)}) collective-permute-start(bf16[32,4224]{1,0:T(8,128)(2,1)S(1)} %collective-permute-done.6), channel_id=1, source_target_pairs={{2,0},{65,1},{4,2},{67,3},{6,4},{69,5},{0,6},{71,7},{10,8},{73,9},... | collective-permute-start | bytes 811016 | tf_op jit(solution)/shard_map/ppermute | solution.py:44
  47.2 2.4 %collective-permute-done.7 = bf16[32,4224]{1,0:T(8,128)(2,1)} collective-permute-done((bf16[32,4224]{1,0:T(8,128)(2,1)S(1)}, bf16[32,4224]{1,0:T(8,128)(2,1)}, u32[]{:S(2)}, u32[]{:S(2)}) %collective-permute-start.7) | collective-permute-done | bytes 270368 | tf_op jit(solution)/shard_map/ppermute | solution.py:44
  49.5 1.2 %collective-permute-start.11 = (bf16[32,4224]{1,0:T(8,128)(2,1)}, bf16[32,4224]{1,0:T(8,128)(2,1)}, u32[]{:S(2)}, u32[]{:S(2)}) collective-permute-start(bf16[32,4224]{1,0:T(8,128)(2,1)} %collective-permute-done.7), channel_id=1, source_target_pairs={{2,0},{65,1},{4,2},{67,3},{6,4},{69,5},{0,6},{71,7},{10,8},{73,9},... | collective-permute-start | bytes 811016 | tf_op jit(solution)/shard_map/ppermute | solution.py:44
  50.8 3.5 %fetch_columns.1 = (bf16[501,4096]{1,0:T(8,128)(2,1)S(1)}, bf16[501,4096]{1,0:T(8,128)(2,1)S(1)}, bf16[64,4096]{1,0:T(8,128)(2,1)S(1)}) custom-call(s32[1]{0:T(128)} %bitcast.2.core, bf16[501,8192]{1,0:T(8,128)(2,1)} %unembed.1, bf16[501,8192]{1,0:T(8,128)(2,1)} %collective-permute-done.12.swapped, bf16[64,8192]{1,0:T(8,128)(2,1)S(1)} %bitcast.59), custom_call_target="tpu_custom_call" | custom-call | bytes 17465344 | tf_op jit(solution)/shard_map/fetch_columns/pallas_call | solution.py:72
  55.4 4.9 %give_scores.1 = (f32[1088,256]{1,0:T(8,128)S(1)}, bf16[2,16,16,4224]{3,2,1,0:T(8,128)(2,1)S(1)}) custom-call(s32[1]{0:T(128)} %bitcast.2.core, s32[16]{0:T(128)S(1)} %stack.107.offsets, bf16[2,2,16,4224]{3,2,1,0:T(8,128)(2,1)S(1)} %bitcast.57, bf16[2,2,16,4224]{3,2,1,0:T(8,128)(2,1)S(1)} %bitcast.58, bf16[2,2,16,4224]{3,2,1,0:T(8,128)(2,1)S(1)} %bitcast.60, ...), custom_call_target="tpu_custom_call" | custom-call | flops 2101346304 | bytes 12402688 | tf_op jit(solution)/shard_map/give_scores/pallas_call | solution.py:168
  60.3 2.1 %collective-permute-start.13 = (f32[1088,256]{1,0:T(8,128)S(1)}, f32[1088,256]{1,0:T(8,128)S(1)}, u32[]{:S(2)}, u32[]{:S(2)}) collective-permute-start(f32[1088,256]{1,0:T(8,128)S(1)} %get-tuple-element.31), channel_id=1, source_target_pairs={{0,1},{1,0},{2,3},{3,2},{4,5},{5,4},{6,7},{7,6},{8,9},{9,8},{10,11... | collective-permute-start | bytes 3342344 | tf_op jit(solution)/shard_map/ppermute | solution.py:48
  62.4 2.5 %keep_scores.1 = (f32[1088,256]{1,0:T(8,128)S(1)}, f32[8,256]{1,0:T(8,128)S(1)}) custom-call(s32[1]{0:T(128)} %bitcast.2.core, bf16[2,16,16,4224]{3,2,1,0:T(8,128)(2,1)S(1)} %get-tuple-element.29.rows, bf16[501,4096]{1,0:T(8,128)(2,1)S(1)} %get-tuple-element.26.refs_10_.u_own, bf16[501,4096]{1,0:T(8,128)(2,1)S(1)} %get-tuple-element.27.refs_11_.u_other, ...), custom_call_target="tpu_custom_call" | custom-call | flops 2101346304 | bytes 8208384 | tf_op jit(solution)/shard_map/keep_scores/pallas_call | solution.py:152
  66.0 9.8 %all-to-all-start.1 = ((f32[128,2,128]{2,1,0:T(2,128)}), f32[128,2,128]{2,1,0:T(2,128)S(1)}, u32[]{:S(2)}, u32[]{:S(2)}) async-start(f32[128,2,128]{2,1,0:T(2,128)} %bitcast.40), calls=%async_computation.1 | async-start | bytes 262144 | tf_op jit(solution)/shard_map/all_to_all | solution.py:371
  77.8 9.6 %all-to-all-done.1 = f32[128,2,128]{2,1,0:T(2,128)S(1)} async-done(((f32[128,2,128]{2,1,0:T(2,128)}), f32[128,2,128]{2,1,0:T(2,128)S(1)}, u32[]{:S(2)}, u32[]{:S(2)}) %all-to-all-start.1) | async-done | bytes 131104 | tf_op jit(solution)/shard_map/all_to_all | solution.py:371
  87.4 2.3 %delta_project.1 = f32[256,128]{1,0:T(8,128)} custom-call(s32[3]{0:T(128)S(1)} %pad_add_fusion.place, f32[1024,256]{1,0:T(8,128)S(1)} %get-tuple-element.32.logits, f32[256,128]{1,0:T(8,128)S(1)} %bitcast.62, f32[8,256]{1,0:T(8,128)S(1)} %get-tuple-element.34.ids, bf16[501,64]{1,0:T(8,128)(2,1)S(1)} %copy.13.op_own, ...), custom_call_target="tpu_custom_call" | custom-call | tf_op jit(solution)/shard_map/delta_project/pallas_call | solution.py:247
  89.7 6.7 %all-to-all-start.2 = ((f32[256,1,128]{2,1,0:T(1,128)}), f32[256,1,128]{2,1,0:T(1,128)S(1)}, u32[]{:S(2)}, u32[]{:S(2)}) async-start(f32[256,1,128]{2,1,0:T(1,128)} %bitcast.43), calls=%async_computation.2 | async-start | bytes 262144 | tf_op jit(solution)/shard_map/all_to_all | solution.py:377
  96.4 2.4 %collective-permute-start.15 = (f32[64,256]{1,0:T(8,128)S(1)}, f32[64,256]{1,0:T(8,128)S(1)}, u32[]{:S(2)}, u32[]{:S(2)}) collective-permute-start(f32[64,256]{1,0:T(8,128)S(1)} %get-tuple-element.36.proj), channel_id=1, source_target_pairs={{0,1},{1,0},{2,3},{3,2},{4,5},{5,4},{6,7},{7,6},{8,9},{9,8},{10,11... | collective-permute-start | bytes 196616 | tf_op jit(solution)/shard_map/ppermute | solution.py:48
  100.5 9.1 %all-to-all-done.2 = f32[256,1,128]{2,1,0:T(1,128)S(1)} async-done(((f32[256,1,128]{2,1,0:T(1,128)}), f32[256,1,128]{2,1,0:T(1,128)S(1)}, u32[]{:S(2)}, u32[]{:S(2)}) %all-to-all-start.2) | async-done | bytes 131104 | tf_op jit(solution)/shard_map/all_to_all | solution.py:377
  (43 shorter events, 10.3 us)
Async XLA Ops:
  0.8 4.2 %collective-permute-start = (bf16[2,4096]{1,0:T(2,128)(2,1)S(1)}, bf16[2,4096]{1,0:T(2,128)(2,1)S(1)}, u32[]{:S(2)}, u32[]{:S(2)}) collective-permute-start(bf16[2,4096]{1,0:T(2,128)(2,1)S(1)} %get-tuple-element.38), channel_id=1, source_target_pairs={{0,1},{1,0},{2,3},{3,2},{4,5},{5,4},{6,7},{7,6},{8,9},{9,8},{10,11... | collective-permute-start | bytes 49160 | tf_op jit(solution)/shard_map/ppermute | solution.py:48
  5.1 45.7 %collective-permute-start.12 = (bf16[501,8192]{1,0:T(8,128)(2,1)}, bf16[501,8192]{1,0:T(8,128)(2,1)}, u32[]{:S(2)}, u32[]{:S(2)}) collective-permute-start(bf16[501,8192]{1,0:T(8,128)(2,1)} %unembed.1), channel_id=1, source_target_pairs={{0,1},{1,0},{2,3},{3,2},{4,5},{5,4},{6,7},{7,6},{8,9},{9,8},{10,11... | collective-permute-start | bytes 24625160 | tf_op jit(solution)/shard_map/ppermute | solution.py:48
  24.3 26.5 %copy-start = (bf16[8192,64]{0,1:T(8,128)(2,1)S(1)}, bf16[8192,64]{0,1:T(8,128)(2,1)}, u32[]{:S(2)}) copy-start(bf16[8192,64]{0,1:T(8,128)(2,1)} %param.9) | copy-start | bytes 3145732
  24.3 6.2 %collective-permute-start.1 = (bf16[32,4224]{1,0:T(8,128)(2,1)S(1)}, bf16[32,4224]{1,0:T(8,128)(2,1)S(1)}, u32[]{:S(2)}, u32[]{:S(2)}) collective-permute-start(bf16[32,4224]{1,0:T(8,128)(2,1)S(1)} %bitcast.65), channel_id=1, source_target_pairs={{64,0},{3,1},{66,2},{5,3},{68,4},{7,5},{70,6},{1,7},{72,8},{11,9},... | collective-permute-start | bytes 811016 | tf_op jit(solution)/shard_map/ppermute | solution.py:44
  27.1 10.3 %collective-permute-start.2 = (bf16[32,4224]{1,0:T(8,128)(2,1)S(1)}, bf16[32,4224]{1,0:T(8,128)(2,1)S(1)}, u32[]{:S(2)}, u32[]{:S(2)}) collective-permute-start(bf16[32,4224]{1,0:T(8,128)(2,1)S(1)} %bitcast.66), channel_id=1, source_target_pairs={{192,0},{7,1},{194,2},{1,3},{196,4},{3,5},{198,6},{5,7},{200,8},{1... | collective-permute-start | bytes 811016 | tf_op jit(solution)/shard_map/ppermute | solution.py:44
  27.1 10.3 %collective-permute-start.3 = (bf16[32,4224]{1,0:T(8,128)(2,1)S(1)}, bf16[32,4224]{1,0:T(8,128)(2,1)S(1)}, u32[]{:S(2)}, u32[]{:S(2)}) collective-permute-start(bf16[32,4224]{1,0:T(8,128)(2,1)S(1)} %bitcast.67), channel_id=1, source_target_pairs={{128,0},{5,1},{130,2},{7,3},{132,4},{1,5},{134,6},{3,7},{136,8},{1... | collective-permute-start | bytes 811016 | tf_op jit(solution)/shard_map/ppermute | solution.py:44
  30.6 13.2 %collective-permute-start.4 = (bf16[64,4224]{1,0:T(8,128)(2,1)S(1)}, bf16[64,4224]{1,0:T(8,128)(2,1)S(1)}, u32[]{:S(2)}, u32[]{:S(2)}) collective-permute-start(bf16[64,4224]{1,0:T(8,128)(2,1)S(1)} %pad_maximum_fusion), channel_id=1, source_target_pairs={{6,0},{193,1},{0,2},{195,3},{2,4},{197,5},{4,6},{199,7},{14,8},{20... | collective-permute-start | bytes 1622024 | tf_op jit(solution)/shard_map/ppermute | solution.py:44
  31.8 12.0 %collective-permute-start.5 = (bf16[64,4224]{1,0:T(8,128)(2,1)S(1)}, bf16[64,4224]{1,0:T(8,128)(2,1)S(1)}, u32[]{:S(2)}, u32[]{:S(2)}) collective-permute-start(bf16[64,4224]{1,0:T(8,128)(2,1)S(1)} %pad_maximum_fusion), channel_id=1, source_target_pairs={{2,0},{65,1},{4,2},{67,3},{6,4},{69,5},{0,6},{71,7},{10,8},{73,9},... | collective-permute-start | bytes 1622024 | tf_op jit(solution)/shard_map/ppermute | solution.py:44
  37.4 16.9 %collective-permute-start.8 = (bf16[64,4224]{1,0:T(8,128)(2,1)S(1)}, bf16[64,4224]{1,0:T(8,128)(2,1)}, u32[]{:S(2)}, u32[]{:S(2)}) collective-permute-start(bf16[64,4224]{1,0:T(8,128)(2,1)S(1)} %constant_dynamic-update-slice_fusion), channel_id=1, source_target_pairs={{6,0},{193,1},{0,2},{195,3},{2,4},{197,5},{4,6},{199,7},{14,8},{20... | collective-permute-start | bytes 1622024 | tf_op jit(solution)/shard_map/ppermute | solution.py:44
  39.0 6.3 %collective-permute-start.6 = (bf16[32,4224]{1,0:T(8,128)(2,1)S(1)}, bf16[32,4224]{1,0:T(8,128)(2,1)S(1)}, u32[]{:S(2)}, u32[]{:S(2)}) collective-permute-start(bf16[32,4224]{1,0:T(8,128)(2,1)S(1)} %collective-permute-done.2), channel_id=1, source_target_pairs={{2,0},{65,1},{4,2},{67,3},{6,4},{69,5},{0,6},{71,7},{10,8},{73,9},... | collective-permute-start | bytes 811016 | tf_op jit(solution)/shard_map/ppermute | solution.py:44
  43.8 5.7 %collective-permute-start.7 = (bf16[32,4224]{1,0:T(8,128)(2,1)S(1)}, bf16[32,4224]{1,0:T(8,128)(2,1)}, u32[]{:S(2)}, u32[]{:S(2)}) collective-permute-start(bf16[32,4224]{1,0:T(8,128)(2,1)S(1)} %collective-permute-done.3), channel_id=1, source_target_pairs={{2,0},{65,1},{4,2},{67,3},{6,4},{69,5},{0,6},{71,7},{10,8},{73,9},... | collective-permute-start | bytes 811016 | tf_op jit(solution)/shard_map/ppermute | solution.py:44
  43.8 11.6 %collective-permute-start.9 = (bf16[64,4224]{1,0:T(8,128)(2,1)S(1)}, bf16[64,4224]{1,0:T(8,128)(2,1)}, u32[]{:S(2)}, u32[]{:S(2)}) collective-permute-start(bf16[64,4224]{1,0:T(8,128)(2,1)S(1)} %collective-permute-done.4), channel_id=1, source_target_pairs={{6,0},{193,1},{0,2},{195,3},{2,4},{197,5},{4,6},{199,7},{14,8},{20... | collective-permute-start | bytes 1622024 | tf_op jit(solution)/shard_map/ppermute | solution.py:44
  45.3 9.0 %collective-permute-start.10 = (bf16[32,4224]{1,0:T(8,128)(2,1)S(1)}, bf16[32,4224]{1,0:T(8,128)(2,1)}, u32[]{:S(2)}, u32[]{:S(2)}) collective-permute-start(bf16[32,4224]{1,0:T(8,128)(2,1)S(1)} %collective-permute-done.6), channel_id=1, source_target_pairs={{2,0},{65,1},{4,2},{67,3},{6,4},{69,5},{0,6},{71,7},{10,8},{73,9},... | collective-permute-start | bytes 811016 | tf_op jit(solution)/shard_map/ppermute | solution.py:44
  49.5 5.9 %collective-permute-start.11 = (bf16[32,4224]{1,0:T(8,128)(2,1)}, bf16[32,4224]{1,0:T(8,128)(2,1)}, u32[]{:S(2)}, u32[]{:S(2)}) collective-permute-start(bf16[32,4224]{1,0:T(8,128)(2,1)} %collective-permute-done.7), channel_id=1, source_target_pairs={{2,0},{65,1},{4,2},{67,3},{6,4},{69,5},{0,6},{71,7},{10,8},{73,9},... | collective-permute-start | bytes 811016 | tf_op jit(solution)/shard_map/ppermute | solution.py:44
  60.3 4.6 %collective-permute-start.13 = (f32[1088,256]{1,0:T(8,128)S(1)}, f32[1088,256]{1,0:T(8,128)S(1)}, u32[]{:S(2)}, u32[]{:S(2)}) collective-permute-start(f32[1088,256]{1,0:T(8,128)S(1)} %get-tuple-element.31), channel_id=1, source_target_pairs={{0,1},{1,0},{2,3},{3,2},{4,5},{5,4},{6,7},{7,6},{8,9},{9,8},{10,11... | collective-permute-start | bytes 3342344 | tf_op jit(solution)/shard_map/ppermute | solution.py:48
  64.9 11.0 %copy-start.1 = (bf16[501,64]{0,1:T(8,128)(2,1)S(1)}, bf16[501,64]{0,1:T(8,128)(2,1)}, u32[]{:S(2)}) copy-start(bf16[501,64]{0,1:T(8,128)(2,1)} %param.8) | copy-start | bytes 192388
  66.0 21.4 %all-to-all-start.1 = ((f32[128,2,128]{2,1,0:T(2,128)}), f32[128,2,128]{2,1,0:T(2,128)S(1)}, u32[]{:S(2)}, u32[]{:S(2)}) async-start(f32[128,2,128]{2,1,0:T(2,128)} %bitcast.40), calls=%async_computation.1 | async-start | bytes 262144 | tf_op jit(solution)/shard_map/all_to_all | solution.py:371
  76.2 1.6 %collective-permute-start.14 = (bf16[501,64]{1,0:T(8,128)(2,1)S(1)}, bf16[501,64]{1,0:T(8,128)(2,1)S(1)}, u32[]{:S(2)}, u32[]{:S(2)}) collective-permute-start(bf16[501,64]{1,0:T(8,128)(2,1)S(1)} %copy.12), channel_id=1, source_target_pairs={{0,1},{1,0},{2,3},{3,2},{4,5},{5,4},{6,7},{7,6},{8,9},{9,8},{10,11... | collective-permute-start | bytes 192392 | tf_op jit(solution)/shard_map/ppermute | solution.py:48
  89.7 19.9 %all-to-all-start.2 = ((f32[256,1,128]{2,1,0:T(1,128)}), f32[256,1,128]{2,1,0:T(1,128)S(1)}, u32[]{:S(2)}, u32[]{:S(2)}) async-start(f32[256,1,128]{2,1,0:T(1,128)} %bitcast.43), calls=%async_computation.2 | async-start | bytes 262144 | tf_op jit(solution)/shard_map/all_to_all | solution.py:377
  96.4 3.3 %collective-permute-start.15 = (f32[64,256]{1,0:T(8,128)S(1)}, f32[64,256]{1,0:T(8,128)S(1)}, u32[]{:S(2)}, u32[]{:S(2)}) collective-permute-start(f32[64,256]{1,0:T(8,128)S(1)} %get-tuple-element.36.proj), channel_id=1, source_target_pairs={{0,1},{1,0},{2,3},{3,2},{4,5},{5,4},{6,7},{7,6},{8,9},{9,8},{10,11... | collective-permute-start | bytes 196616 | tf_op jit(solution)/shard_map/ppermute | solution.py:48

commit v5 on v4

--- a/solution.py
+++ b/solution.py
@@ -231,16 +231,22 @@
         delta = (weight - onehot).astype(jnp.bfloat16)
         projected += lax.dot_general(op[...], delta, CONTRACT_FIRST, preferred_element_type=jnp.float32)
     coords[:, :width] = projected.T
-    lane = lax.broadcasted_iota(jnp.int32, (NZ, 128), 1)
+    coords[:, width:] = jnp.zeros((SIDE, 128 - width), jnp.float32)
     core = place[2]
+    coords[...] = pltpu.roll(coords[...], core * width, 1)
+    group = lax.broadcasted_iota(jnp.int32, (NZ, 128), 1) // 8 - core * 8
+    chosen = [group == u for u in range(8)]
     for x in range(NX):
         pieces = []
         for u in range(8):
             start = x * NY * PIECE + u * NZ
             pieces.append(coords[start : start + NZ, :])
         for r in range(8):
-            line = jnp.concatenate([piece[:, 8 * r : 8 * r + 8] for piece in pieces] * 2, axis=1)
-            out[r * 32 + x * NZ : r * 32 + (x + 1) * NZ, :] = jnp.where(lane // 64 == core, line, 0.0)
+            line = jnp.zeros((NZ, 128), jnp.float32)
+            for u in range(8):
+                moved = pieces[u] if u == r else pltpu.roll(pieces[u], (u - r) * 8 % 128, 1)
+                line = jnp.where(chosen[u], moved, line)
+            out[r * 32 + x * NZ : r * 32 + (x + 1) * NZ, :] = line
 
 
 def delta_project(place, logits, got, ids, op_own, op_other):

time: 111 us -> 111 us (level)
  no operation moved by 1% of the time
where the time goes in v5:
time: 111 us; the launch traced here: 110 us
  starting transfers between devices  39.9 us (36%)
  waiting for transfers between devices  33.3 us (30%)
  blocking collectives  18.7 us (17%)
  Pallas kernels  15.7 us (14%)
  local copies, waits for them, and re-layouts  1.41 us (1%)
    all_to_all x1, blocking collectives, body(): lax.all_to_all(jnp.broadcast_to(chip[None], (NZ,) + chip.shape), 'z', 0, 0)  18.7 us
    ppermute x11, starting transfers between devices, from_shift(): return lax.ppermute(value, ALL, shift_pairs(axes, shift))  14.5 us
    ppermute x11, waiting for transfers between devices, from_shift(): return lax.ppermute(value, ALL, shift_pairs(axes, shift))  12.9 us
    all_to_all x1, starting transfers between devices, body(): got = lax.all_to_all(message, ('x', 'y', 'z'), 0, 0, tiled=True)  9.85 us
    all_to_all x1, waiting for transfers between devices, body(): got = lax.all_to_all(message, ('x', 'y', 'z'), 0, 0, tiled=True)  9.59 us
    all_to_all x1, waiting for transfers between devices, body(): got = lax.all_to_all(sent, ('y', 'c', 'x', 'z'), 0, 0, tiled=True)  9.06 us
    ppermute x5, starting transfers between devices, swap_core(): return lax.ppermute(value, 'c', [(0, 1), (1, 0)])  8.79 us
    all_to_all x1, starting transfers between devices, body(): got = lax.all_to_all(sent, ('y', 'c', 'x', 'z'), 0, 0, tiled=True)  6.7 us
  transfers between devices with their start and end apart: 18, of which 10 were waited for; matrix products, arithmetic and copies ran while one was open for 1% of the time, Pallas kernels for 6%

profile of v5, /device:TPU:1, one launch (start us, length us, event | category | flops | bytes accessed | tf_op | source)
XLA Modules:
  0.0 110.2 jit_solution(6152787500281517911)
XLA Ops:
  0.8 3.3 %collective-permute-start = (bf16[2,4096]{1,0:T(2,128)(2,1)S(1)}, bf16[2,4096]{1,0:T(2,128)(2,1)S(1)}, u32[]{:S(2)}, u32[]{:S(2)}) collective-permute-start(bf16[2,4096]{1,0:T(2,128)(2,1)S(1)} %get-tuple-element.38), channel_id=1, source_target_pairs={{0,1},{1,0},{2,3},{3,2},{4,5},{5,4},{6,7},{7,6},{8,9},{9,8},{10,11... | collective-permute-start | bytes 49160 | tf_op jit(solution)/shard_map/ppermute | solution.py:48
  5.6 18.7 %all_to_all.27 = bf16[8,4,4224]{2,1,0:T(4,128)(2,1)S(1)} all-to-all(bf16[8,4,4224]{2,1,0:T(4,128)(2,1)S(1)} %broadcast_in_dim.32), channel_id=1, replica_groups=mesh['x'=4,'z'=8,'y'=4,'c'=2] {'z'}, dimensions={0} | all-to-all | bytes 540672 | tf_op jit(solution)/shard_map/all_to_all | solution.py:333
  24.3 2.8 %collective-permute-start.1 = (bf16[32,4224]{1,0:T(8,128)(2,1)S(1)}, bf16[32,4224]{1,0:T(8,128)(2,1)S(1)}, u32[]{:S(2)}, u32[]{:S(2)}) collective-permute-start(bf16[32,4224]{1,0:T(8,128)(2,1)S(1)} %bitcast.65), channel_id=1, source_target_pairs={{64,0},{3,1},{66,2},{5,3},{68,4},{7,5},{70,6},{1,7},{72,8},{11,9},... | collective-permute-start | bytes 811016 | tf_op jit(solution)/shard_map/ppermute | solution.py:44
  27.1 1.6 %collective-permute-start.3 = (bf16[32,4224]{1,0:T(8,128)(2,1)S(1)}, bf16[32,4224]{1,0:T(8,128)(2,1)S(1)}, u32[]{:S(2)}, u32[]{:S(2)}) collective-permute-start(bf16[32,4224]{1,0:T(8,128)(2,1)S(1)} %bitcast.67), channel_id=1, source_target_pairs={{128,0},{5,1},{130,2},{7,3},{132,4},{1,5},{134,6},{3,7},{136,8},{1... | collective-permute-start | bytes 811016 | tf_op jit(solution)/shard_map/ppermute | solution.py:44
  28.8 1.8 %collective-permute-done.1 = bf16[32,4224]{1,0:T(8,128)(2,1)S(1)} collective-permute-done((bf16[32,4224]{1,0:T(8,128)(2,1)S(1)}, bf16[32,4224]{1,0:T(8,128)(2,1)S(1)}, u32[]{:S(2)}, u32[]{:S(2)}) %collective-permute-start.1) | collective-permute-done | bytes 270368 | tf_op jit(solution)/shard_map/ppermute | solution.py:44
  30.6 1.3 %collective-permute-start.4 = (bf16[64,4224]{1,0:T(8,128)(2,1)S(1)}, bf16[64,4224]{1,0:T(8,128)(2,1)S(1)}, u32[]{:S(2)}, u32[]{:S(2)}) collective-permute-start(bf16[64,4224]{1,0:T(8,128)(2,1)S(1)} %pad_maximum_fusion), channel_id=1, source_target_pairs={{6,0},{193,1},{0,2},{195,3},{2,4},{197,5},{4,6},{199,7},{14,8},{20... | collective-permute-start | bytes 1622024 | tf_op jit(solution)/shard_map/ppermute | solution.py:44
  31.8 1.5 %collective-permute-start.5 = (bf16[64,4224]{1,0:T(8,128)(2,1)S(1)}, bf16[64,4224]{1,0:T(8,128)(2,1)S(1)}, u32[]{:S(2)}, u32[]{:S(2)}) collective-permute-start(bf16[64,4224]{1,0:T(8,128)(2,1)S(1)} %pad_maximum_fusion), channel_id=1, source_target_pairs={{2,0},{65,1},{4,2},{67,3},{6,4},{69,5},{0,6},{71,7},{10,8},{73,9},... | collective-permute-start | bytes 1622024 | tf_op jit(solution)/shard_map/ppermute | solution.py:44
  33.3 4.1 %collective-permute-done.2 = bf16[32,4224]{1,0:T(8,128)(2,1)S(1)} collective-permute-done((bf16[32,4224]{1,0:T(8,128)(2,1)S(1)}, bf16[32,4224]{1,0:T(8,128)(2,1)S(1)}, u32[]{:S(2)}, u32[]{:S(2)}) %collective-permute-start.2) | collective-permute-done | bytes 270368 | tf_op jit(solution)/shard_map/ppermute | solution.py:44
  37.4 1.6 %collective-permute-start.8 = (bf16[64,4224]{1,0:T(8,128)(2,1)S(1)}, bf16[64,4224]{1,0:T(8,128)(2,1)}, u32[]{:S(2)}, u32[]{:S(2)}) collective-permute-start(bf16[64,4224]{1,0:T(8,128)(2,1)S(1)} %constant_dynamic-update-slice_fusion), channel_id=1, source_target_pairs={{6,0},{193,1},{0,2},{195,3},{2,4},{197,5},{4,6},{199,7},{14,8},{20... | collective-permute-start | bytes 1622024 | tf_op jit(solution)/shard_map/ppermute | solution.py:44
  40.2 3.6 %collective-permute-done.4 = bf16[64,4224]{1,0:T(8,128)(2,1)S(1)} collective-permute-done((bf16[64,4224]{1,0:T(8,128)(2,1)S(1)}, bf16[64,4224]{1,0:T(8,128)(2,1)S(1)}, u32[]{:S(2)}, u32[]{:S(2)}) %collective-permute-start.4) | collective-permute-done | bytes 540704 | tf_op jit(solution)/shard_map/ppermute | solution.py:44
  43.8 1.5 %collective-permute-start.9 = (bf16[64,4224]{1,0:T(8,128)(2,1)S(1)}, bf16[64,4224]{1,0:T(8,128)(2,1)}, u32[]{:S(2)}, u32[]{:S(2)}) collective-permute-start(bf16[64,4224]{1,0:T(8,128)(2,1)S(1)} %collective-permute-done.4), channel_id=1, source_target_pairs={{6,0},{193,1},{0,2},{195,3},{2,4},{197,5},{4,6},{199,7},{14,8},{20... | collective-permute-start | bytes 1622024 | tf_op jit(solution)/shard_map/ppermute | solution.py:44
  45.3 1.9 %collective-permute-start.10 = (bf16[32,4224]{1,0:T(8,128)(2,1)S(1)}, bf16[32,4224]{1,0:T(8,128)(2,1)}, u32[]{:S(2)}, u32[]{:S(2)}) collective-permute-start(bf16[32,4224]{1,0:T(8,128)(2,1)S(1)} %collective-permute-done.6), channel_id=1, source_target_pairs={{2,0},{65,1},{4,2},{67,3},{6,4},{69,5},{0,6},{71,7},{10,8},{73,9},... | collective-permute-start | bytes 811016 | tf_op jit(solution)/shard_map/ppermute | solution.py:44
  47.2 2.4 %collective-permute-done.7 = bf16[32,4224]{1,0:T(8,128)(2,1)} collective-permute-done((bf16[32,4224]{1,0:T(8,128)(2,1)S(1)}, bf16[32,4224]{1,0:T(8,128)(2,1)}, u32[]{:S(2)}, u32[]{:S(2)}) %collective-permute-start.7) | collective-permute-done | bytes 270368 | tf_op jit(solution)/shard_map/ppermute | solution.py:44
  49.5 1.2 %collective-permute-start.11 = (bf16[32,4224]{1,0:T(8,128)(2,1)}, bf16[32,4224]{1,0:T(8,128)(2,1)}, u32[]{:S(2)}, u32[]{:S(2)}) collective-permute-start(bf16[32,4224]{1,0:T(8,128)(2,1)} %collective-permute-done.7), channel_id=1, source_target_pairs={{2,0},{65,1},{4,2},{67,3},{6,4},{69,5},{0,6},{71,7},{10,8},{73,9},... | collective-permute-start | bytes 811016 | tf_op jit(solution)/shard_map/ppermute | solution.py:44
  50.8 3.5 %fetch_columns.1 = (bf16[501,4096]{1,0:T(8,128)(2,1)S(1)}, bf16[501,4096]{1,0:T(8,128)(2,1)S(1)}, bf16[64,4096]{1,0:T(8,128)(2,1)S(1)}) custom-call(s32[1]{0:T(128)} %bitcast.2.core, bf16[501,8192]{1,0:T(8,128)(2,1)} %unembed.1, bf16[501,8192]{1,0:T(8,128)(2,1)} %collective-permute-done.12.swapped, bf16[64,8192]{1,0:T(8,128)(2,1)S(1)} %bitcast.59), custom_call_target="tpu_custom_call" | custom-call | bytes 17465344 | tf_op jit(solution)/shard_map/fetch_columns/pallas_call | solution.py:72
  55.4 4.9 %give_scores.1 = (f32[1088,256]{1,0:T(8,128)S(1)}, bf16[2,16,16,4224]{3,2,1,0:T(8,128)(2,1)S(1)}) custom-call(s32[1]{0:T(128)} %bitcast.2.core, s32[16]{0:T(128)S(1)} %stack.107.offsets, bf16[2,2,16,4224]{3,2,1,0:T(8,128)(2,1)S(1)} %bitcast.57, bf16[2,2,16,4224]{3,2,1,0:T(8,128)(2,1)S(1)} %bitcast.58, bf16[2,2,16,4224]{3,2,1,0:T(8,128)(2,1)S(1)} %bitcast.60, ...), custom_call_target="tpu_custom_call" | custom-call | flops 2101346304 | bytes 12402688 | tf_op jit(solution)/shard_map/give_scores/pallas_call | solution.py:168
  60.3 2.1 %collective-permute-start.13 = (f32[1088,256]{1,0:T(8,128)S(1)}, f32[1088,256]{1,0:T(8,128)S(1)}, u32[]{:S(2)}, u32[]{:S(2)}) collective-permute-start(f32[1088,256]{1,0:T(8,128)S(1)} %get-tuple-element.31), channel_id=1, source_target_pairs={{0,1},{1,0},{2,3},{3,2},{4,5},{5,4},{6,7},{7,6},{8,9},{9,8},{10,11... | collective-permute-start | bytes 3342344 | tf_op jit(solution)/shard_map/ppermute | solution.py:48
  62.4 2.5 %keep_scores.1 = (f32[1088,256]{1,0:T(8,128)S(1)}, f32[8,256]{1,0:T(8,128)S(1)}) custom-call(s32[1]{0:T(128)} %bitcast.2.core, bf16[2,16,16,4224]{3,2,1,0:T(8,128)(2,1)S(1)} %get-tuple-element.29.rows, bf16[501,4096]{1,0:T(8,128)(2,1)S(1)} %get-tuple-element.26.refs_10_.u_own, bf16[501,4096]{1,0:T(8,128)(2,1)S(1)} %get-tuple-element.27.refs_11_.u_other, ...), custom_call_target="tpu_custom_call" | custom-call | flops 2101346304 | bytes 8208384 | tf_op jit(solution)/shard_map/keep_scores/pallas_call | solution.py:152
  66.0 9.8 %all-to-all-start.1 = ((f32[128,2,128]{2,1,0:T(2,128)}), f32[128,2,128]{2,1,0:T(2,128)S(1)}, u32[]{:S(2)}, u32[]{:S(2)}) async-start(f32[128,2,128]{2,1,0:T(2,128)} %bitcast.40), calls=%async_computation.1 | async-start | bytes 262144 | tf_op jit(solution)/shard_map/all_to_all | solution.py:377
  77.8 9.6 %all-to-all-done.1 = f32[128,2,128]{2,1,0:T(2,128)S(1)} async-done(((f32[128,2,128]{2,1,0:T(2,128)}), f32[128,2,128]{2,1,0:T(2,128)S(1)}, u32[]{:S(2)}, u32[]{:S(2)}) %all-to-all-start.1) | async-done | bytes 131104 | tf_op jit(solution)/shard_map/all_to_all | solution.py:377
  87.4 2.1 %delta_project.1 = f32[256,128]{1,0:T(8,128)} custom-call(s32[3]{0:T(128)S(1)} %pad_add_fusion.place, f32[1024,256]{1,0:T(8,128)S(1)} %get-tuple-element.32.logits, f32[256,128]{1,0:T(8,128)S(1)} %bitcast.62, f32[8,256]{1,0:T(8,128)S(1)} %get-tuple-element.34.ids, bf16[501,64]{1,0:T(8,128)(2,1)S(1)} %copy.13.op_own, ...), custom_call_target="tpu_custom_call" | custom-call | tf_op jit(solution)/shard_map/delta_project/pallas_call | solution.py:253
  89.5 6.7 %all-to-all-start.2 = ((f32[256,1,128]{2,1,0:T(1,128)}), f32[256,1,128]{2,1,0:T(1,128)S(1)}, u32[]{:S(2)}, u32[]{:S(2)}) async-start(f32[256,1,128]{2,1,0:T(1,128)} %bitcast.43), calls=%async_computation.2 | async-start | bytes 262144 | tf_op jit(solution)/shard_map/all_to_all | solution.py:383
  96.2 2.4 %collective-permute-start.15 = (f32[64,256]{1,0:T(8,128)S(1)}, f32[64,256]{1,0:T(8,128)S(1)}, u32[]{:S(2)}, u32[]{:S(2)}) collective-permute-start(f32[64,256]{1,0:T(8,128)S(1)} %get-tuple-element.36.proj), channel_id=1, source_target_pairs={{0,1},{1,0},{2,3},{3,2},{4,5},{5,4},{6,7},{7,6},{8,9},{9,8},{10,11... | collective-permute-start | bytes 196616 | tf_op jit(solution)/shard_map/ppermute | solution.py:48
  100.3 9.1 %all-to-all-done.2 = f32[256,1,128]{2,1,0:T(1,128)S(1)} async-done(((f32[256,1,128]{2,1,0:T(1,128)}), f32[256,1,128]{2,1,0:T(1,128)S(1)}, u32[]{:S(2)}, u32[]{:S(2)}) %all-to-all-start.2) | async-done | bytes 131104 | tf_op jit(solution)/shard_map/all_to_all | solution.py:383
  (43 shorter events, 10.3 us)
Async XLA Ops:
  0.8 4.2 %collective-permute-start = (bf16[2,4096]{1,0:T(2,128)(2,1)S(1)}, bf16[2,4096]{1,0:T(2,128)(2,1)S(1)}, u32[]{:S(2)}, u32[]{:S(2)}) collective-permute-start(bf16[2,4096]{1,0:T(2,128)(2,1)S(1)} %get-tuple-element.38), channel_id=1, source_target_pairs={{0,1},{1,0},{2,3},{3,2},{4,5},{5,4},{6,7},{7,6},{8,9},{9,8},{10,11... | collective-permute-start | bytes 49160 | tf_op jit(solution)/shard_map/ppermute | solution.py:48
  5.1 45.7 %collective-permute-start.12 = (bf16[501,8192]{1,0:T(8,128)(2,1)}, bf16[501,8192]{1,0:T(8,128)(2,1)}, u32[]{:S(2)}, u32[]{:S(2)}) collective-permute-start(bf16[501,8192]{1,0:T(8,128)(2,1)} %unembed.1), channel_id=1, source_target_pairs={{0,1},{1,0},{2,3},{3,2},{4,5},{5,4},{6,7},{7,6},{8,9},{9,8},{10,11... | collective-permute-start | bytes 24625160 | tf_op jit(solution)/shard_map/ppermute | solution.py:48
  24.3 26.5 %copy-start = (bf16[8192,64]{0,1:T(8,128)(2,1)S(1)}, bf16[8192,64]{0,1:T(8,128)(2,1)}, u32[]{:S(2)}) copy-start(bf16[8192,64]{0,1:T(8,128)(2,1)} %param.9) | copy-start | bytes 3145732
  24.3 6.2 %collective-permute-start.1 = (bf16[32,4224]{1,0:T(8,128)(2,1)S(1)}, bf16[32,4224]{1,0:T(8,128)(2,1)S(1)}, u32[]{:S(2)}, u32[]{:S(2)}) collective-permute-start(bf16[32,4224]{1,0:T(8,128)(2,1)S(1)} %bitcast.65), channel_id=1, source_target_pairs={{64,0},{3,1},{66,2},{5,3},{68,4},{7,5},{70,6},{1,7},{72,8},{11,9},... | collective-permute-start | bytes 811016 | tf_op jit(solution)/shard_map/ppermute | solution.py:44
  27.1 10.3 %collective-permute-start.2 = (bf16[32,4224]{1,0:T(8,128)(2,1)S(1)}, bf16[32,4224]{1,0:T(8,128)(2,1)S(1)}, u32[]{:S(2)}, u32[]{:S(2)}) collective-permute-start(bf16[32,4224]{1,0:T(8,128)(2,1)S(1)} %bitcast.66), channel_id=1, source_target_pairs={{192,0},{7,1},{194,2},{1,3},{196,4},{3,5},{198,6},{5,7},{200,8},{1... | collective-permute-start | bytes 811016 | tf_op jit(solution)/shard_map/ppermute | solution.py:44
  27.1 10.3 %collective-permute-start.3 = (bf16[32,4224]{1,0:T(8,128)(2,1)S(1)}, bf16[32,4224]{1,0:T(8,128)(2,1)S(1)}, u32[]{:S(2)}, u32[]{:S(2)}) collective-permute-start(bf16[32,4224]{1,0:T(8,128)(2,1)S(1)} %bitcast.67), channel_id=1, source_target_pairs={{128,0},{5,1},{130,2},{7,3},{132,4},{1,5},{134,6},{3,7},{136,8},{1... | collective-permute-start | bytes 811016 | tf_op jit(solution)/shard_map/ppermute | solution.py:44
  30.6 13.2 %collective-permute-start.4 = (bf16[64,4224]{1,0:T(8,128)(2,1)S(1)}, bf16[64,4224]{1,0:T(8,128)(2,1)S(1)}, u32[]{:S(2)}, u32[]{:S(2)}) collective-permute-start(bf16[64,4224]{1,0:T(8,128)(2,1)S(1)} %pad_maximum_fusion), channel_id=1, source_target_pairs={{6,0},{193,1},{0,2},{195,3},{2,4},{197,5},{4,6},{199,7},{14,8},{20... | collective-permute-start | bytes 1622024 | tf_op jit(solution)/shard_map/ppermute | solution.py:44
  31.8 12.0 %collective-permute-start.5 = (bf16[64,4224]{1,0:T(8,128)(2,1)S(1)}, bf16[64,4224]{1,0:T(8,128)(2,1)S(1)}, u32[]{:S(2)}, u32[]{:S(2)}) collective-permute-start(bf16[64,4224]{1,0:T(8,128)(2,1)S(1)} %pad_maximum_fusion), channel_id=1, source_target_pairs={{2,0},{65,1},{4,2},{67,3},{6,4},{69,5},{0,6},{71,7},{10,8},{73,9},... | collective-permute-start | bytes 1622024 | tf_op jit(solution)/shard_map/ppermute | solution.py:44
  37.4 16.9 %collective-permute-start.8 = (bf16[64,4224]{1,0:T(8,128)(2,1)S(1)}, bf16[64,4224]{1,0:T(8,128)(2,1)}, u32[]{:S(2)}, u32[]{:S(2)}) collective-permute-start(bf16[64,4224]{1,0:T(8,128)(2,1)S(1)} %constant_dynamic-update-slice_fusion), channel_id=1, source_target_pairs={{6,0},{193,1},{0,2},{195,3},{2,4},{197,5},{4,6},{199,7},{14,8},{20... | collective-permute-start | bytes 1622024 | tf_op jit(solution)/shard_map/ppermute | solution.py:44
  39.0 6.3 %collective-permute-start.6 = (bf16[32,4224]{1,0:T(8,128)(2,1)S(1)}, bf16[32,4224]{1,0:T(8,128)(2,1)S(1)}, u32[]{:S(2)}, u32[]{:S(2)}) collective-permute-start(bf16[32,4224]{1,0:T(8,128)(2,1)S(1)} %collective-permute-done.2), channel_id=1, source_target_pairs={{2,0},{65,1},{4,2},{67,3},{6,4},{69,5},{0,6},{71,7},{10,8},{73,9},... | collective-permute-start | bytes 811016 | tf_op jit(solution)/shard_map/ppermute | solution.py:44
  43.8 5.7 %collective-permute-start.7 = (bf16[32,4224]{1,0:T(8,128)(2,1)S(1)}, bf16[32,4224]{1,0:T(8,128)(2,1)}, u32[]{:S(2)}, u32[]{:S(2)}) collective-permute-start(bf16[32,4224]{1,0:T(8,128)(2,1)S(1)} %collective-permute-done.3), channel_id=1, source_target_pairs={{2,0},{65,1},{4,2},{67,3},{6,4},{69,5},{0,6},{71,7},{10,8},{73,9},... | collective-permute-start | bytes 811016 | tf_op jit(solution)/shard_map/ppermute | solution.py:44
  43.8 11.6 %collective-permute-start.9 = (bf16[64,4224]{1,0:T(8,128)(2,1)S(1)}, bf16[64,4224]{1,0:T(8,128)(2,1)}, u32[]{:S(2)}, u32[]{:S(2)}) collective-permute-start(bf16[64,4224]{1,0:T(8,128)(2,1)S(1)} %collective-permute-done.4), channel_id=1, source_target_pairs={{6,0},{193,1},{0,2},{195,3},{2,4},{197,5},{4,6},{199,7},{14,8},{20... | collective-permute-start | bytes 1622024 | tf_op jit(solution)/shard_map/ppermute | solution.py:44
  45.3 9.0 %collective-permute-start.10 = (bf16[32,4224]{1,0:T(8,128)(2,1)S(1)}, bf16[32,4224]{1,0:T(8,128)(2,1)}, u32[]{:S(2)}, u32[]{:S(2)}) collective-permute-start(bf16[32,4224]{1,0:T(8,128)(2,1)S(1)} %collective-permute-done.6), channel_id=1, source_target_pairs={{2,0},{65,1},{4,2},{67,3},{6,4},{69,5},{0,6},{71,7},{10,8},{73,9},... | collective-permute-start | bytes 811016 | tf_op jit(solution)/shard_map/ppermute | solution.py:44
  49.5 5.9 %collective-permute-start.11 = (bf16[32,4224]{1,0:T(8,128)(2,1)}, bf16[32,4224]{1,0:T(8,128)(2,1)}, u32[]{:S(2)}, u32[]{:S(2)}) collective-permute-start(bf16[32,4224]{1,0:T(8,128)(2,1)} %collective-permute-done.7), channel_id=1, source_target_pairs={{2,0},{65,1},{4,2},{67,3},{6,4},{69,5},{0,6},{71,7},{10,8},{73,9},... | collective-permute-start | bytes 811016 | tf_op jit(solution)/shard_map/ppermute | solution.py:44
  60.3 4.6 %collective-permute-start.13 = (f32[1088,256]{1,0:T(8,128)S(1)}, f32[1088,256]{1,0:T(8,128)S(1)}, u32[]{:S(2)}, u32[]{:S(2)}) collective-permute-start(f32[1088,256]{1,0:T(8,128)S(1)} %get-tuple-element.31), channel_id=1, source_target_pairs={{0,1},{1,0},{2,3},{3,2},{4,5},{5,4},{6,7},{7,6},{8,9},{9,8},{10,11... | collective-permute-start | bytes 3342344 | tf_op jit(solution)/shard_map/ppermute | solution.py:48
  64.9 11.0 %copy-start.1 = (bf16[501,64]{0,1:T(8,128)(2,1)S(1)}, bf16[501,64]{0,1:T(8,128)(2,1)}, u32[]{:S(2)}) copy-start(bf16[501,64]{0,1:T(8,128)(2,1)} %param.8) | copy-start | bytes 192388
  66.0 21.4 %all-to-all-start.1 = ((f32[128,2,128]{2,1,0:T(2,128)}), f32[128,2,128]{2,1,0:T(2,128)S(1)}, u32[]{:S(2)}, u32[]{:S(2)}) async-start(f32[128,2,128]{2,1,0:T(2,128)} %bitcast.40), calls=%async_computation.1 | async-start | bytes 262144 | tf_op jit(solution)/shard_map/all_to_all | solution.py:377
  76.2 1.6 %collective-permute-start.14 = (bf16[501,64]{1,0:T(8,128)(2,1)S(1)}, bf16[501,64]{1,0:T(8,128)(2,1)S(1)}, u32[]{:S(2)}, u32[]{:S(2)}) collective-permute-start(bf16[501,64]{1,0:T(8,128)(2,1)S(1)} %copy.12), channel_id=1, source_target_pairs={{0,1},{1,0},{2,3},{3,2},{4,5},{5,4},{6,7},{7,6},{8,9},{9,8},{10,11... | collective-permute-start | bytes 192392 | tf_op jit(solution)/shard_map/ppermute | solution.py:48
  89.5 19.9 %all-to-all-start.2 = ((f32[256,1,128]{2,1,0:T(1,128)}), f32[256,1,128]{2,1,0:T(1,128)S(1)}, u32[]{:S(2)}, u32[]{:S(2)}) async-start(f32[256,1,128]{2,1,0:T(1,128)} %bitcast.43), calls=%async_computation.2 | async-start | bytes 262144 | tf_op jit(solution)/shard_map/all_to_all | solution.py:383
  96.2 3.3 %collective-permute-start.15 = (f32[64,256]{1,0:T(8,128)S(1)}, f32[64,256]{1,0:T(8,128)S(1)}, u32[]{:S(2)}, u32[]{:S(2)}) collective-permute-start(f32[64,256]{1,0:T(8,128)S(1)} %get-tuple-element.36.proj), channel_id=1, source_target_pairs={{0,1},{1,0},{2,3},{3,2},{4,5},{5,4},{6,7},{7,6},{8,9},{9,8},{10,11... | collective-permute-start | bytes 196616 | tf_op jit(solution)/shard_map/ppermute | solution.py:48
